TPU v7x, 32 devices: a whole 2x2x4 slice. The times are simulated.
32 devices in a mesh: section: 16 (over z, x, core), tp: 2 (over y).
Axes of the slice: x: 2, y: 2, z: 4, core: 2. Of those that a mesh axis runs over, the one named last changes fastest.
Arguments:
- fwd_q: bfloat16 [16, 128, 8192], P('section', None, 'tp'), may hold values from -4.5 to 4.5
- fwd_k: bfloat16 [16, 128, 1024], P('section', None, 'tp'), may hold values from -4.5 to 4.5
- fwd_v: bfloat16 [16, 128, 1024], P('section', None, 'tp'), may hold values from -6 to 6
- fwd_segments: int32 [16, 128], P('section'), may hold values from 0 to 3, never falling along the last dimension, each value on 1 to 64 neighbouring positions
- held_q: bfloat16 [16, 128, 8192], P('section', None, 'tp'), may hold values from -4.5 to 4.5
- held_k: bfloat16 [16, 128, 1024], P('section', None, 'tp'), may hold values from -4.5 to 4.5
- held_v: bfloat16 [16, 128, 1024], P('section', None, 'tp'), may hold values from -6 to 6
- back_segments: int32 [16, 128], P('section'), may hold values from 0 to 3, never falling along the last dimension, each value on 1 to 64 neighbouring positions
- up_grad: bfloat16 [16, 128, 8192], P('section', None, 'tp'), may hold values from -6 to 6
Outputs:
- passed_output: bfloat16 [16, 128, 8192], P('section', 'tp')
- evicted_q: bfloat16 [16, 128, 8192], P('section', None, 'tp')
- evicted_k: bfloat16 [16, 128, 1024], P('section', None, 'tp')
- evicted_v: bfloat16 [16, 128, 1024], P('section', None, 'tp')
- grad_q: bfloat16 [16, 128, 8192], P('section', None, 'tp')
- grad_k: bfloat16 [16, 128, 1024], P('section', None, 'tp')
- grad_v: bfloat16 [16, 128, 1024], P('section', None, 'tp')
Inputs may be any that keep to these rules, and one draw needn't show every extreme that they name: `fwd_segments`: document numbers never fall along a micro-batch; each document has 1 to 64 tokens. `back_segments`: document numbers never fall along a micro-batch; each document has 1 to 64 tokens.
All inputs are finite; a program needn't handle non-finite values.
Results may differ from a plain program's by a relative error of at most 0.0058.
Values may be sent and summed in bfloat16 or wider, within the bound.
A program may use at most 64 MiB of HBM per device.

v0:
```python
import jax
import jax.numpy as jnp
from jax import lax
from jax.sharding import PartitionSpec as P

HQ = 64
KV = 8
HD = 128


def shifted_2(value, axis, steps):
    count = lax.axis_size(axis)
    pairs = [(source, (source + steps) % count) for source in range(count)]
    return lax.ppermute(value, axis, pairs)


def split_heads(queries, key_rows, value_rows):
    row_count = queries.shape[0]
    kv_local = key_rows.shape[1] // HD
    group_size = HQ // KV
    query_heads = queries.reshape(row_count, kv_local, group_size, HD)
    key_heads = key_rows.reshape(row_count, kv_local, HD)
    value_heads = value_rows.reshape(row_count, kv_local, HD)
    return (query_heads, key_heads, value_heads)


def probability(query_heads, key_heads, segment_ids):
    row_count = query_heads.shape[0]
    scores = jnp.einsum(
        "qkgd,skd->kgqs", query_heads, key_heads, preferred_element_type=jnp.float32
    ) * HD ** (-0.5)
    positions = jnp.arange(row_count)
    allowed = (segment_ids[:, None] == segment_ids[None, :]) & (
        positions[:, None] >= positions[None, :]
    )
    scores = jnp.where(allowed, scores, -jnp.inf)
    row_max = jnp.max(scores, axis=-1, keepdims=True)
    weights = jnp.exp(scores - row_max)
    return weights / jnp.sum(weights, axis=-1, keepdims=True)


def forward(queries, key_rows, value_rows, segment_ids):
    query_heads, key_heads, value_heads = split_heads(queries, key_rows, value_rows)
    prob = probability(query_heads, key_heads, segment_ids)
    prob_low = prob.astype(jnp.bfloat16)
    result = jnp.einsum("kgqs,skd->qkgd", prob_low, value_heads, preferred_element_type=jnp.float32)
    return result.reshape(queries.shape[0], queries.shape[1]).astype(jnp.bfloat16)


def backward(queries, key_rows, value_rows, segment_ids, out_grad):
    row_count = queries.shape[0]
    query_heads, key_heads, value_heads = split_heads(queries, key_rows, value_rows)
    prob = probability(query_heads, key_heads, segment_ids)
    prob_low = prob.astype(jnp.bfloat16)
    grad_heads = out_grad.reshape(query_heads.shape)
    value_grad = jnp.einsum(
        "kgqs,qkgd->skd", prob_low, grad_heads, preferred_element_type=jnp.float32
    )
    dprob = jnp.einsum(
        "qkgd,skd->kgqs", grad_heads, value_heads, preferred_element_type=jnp.float32
    )
    delta = jnp.sum(prob * dprob, axis=-1, keepdims=True)
    dscore = (prob * (dprob - delta) * HD ** (-0.5)).astype(jnp.bfloat16)
    query_grad = jnp.einsum("kgqs,skd->qkgd", dscore, key_heads, preferred_element_type=jnp.float32)
    key_grad = jnp.einsum("kgqs,qkgd->skd", dscore, query_heads, preferred_element_type=jnp.float32)
    return (
        query_grad.reshape(row_count, queries.shape[1]).astype(jnp.bfloat16),
        key_grad.reshape(row_count, key_rows.shape[1]).astype(jnp.bfloat16),
        value_grad.reshape(row_count, key_rows.shape[1]).astype(jnp.bfloat16),
    )


def mirror_move(stash):
    section_count = lax.axis_size("section")
    row_count = stash.shape[0]
    width = stash.shape[1]
    pieces = stash.reshape(row_count, section_count, width // section_count)
    spread = lax.all_to_all(pieces, "section", split_axis=1, concat_axis=1, tiled=True)
    flipped = jnp.flip(spread, axis=1)
    collected = lax.all_to_all(flipped, "section", split_axis=1, concat_axis=1, tiled=True)
    return collected.reshape(row_count, width)


def shards(fwd_q, fwd_k, fwd_v, fwd_segments, held_q, held_k, held_v, back_segments, up_grad):
    query_width = fwd_q.shape[2]
    key_width = fwd_k.shape[2]
    held_stash = jnp.concatenate([held_q[0], held_k[0], held_v[0]], axis=1)
    held_stash = mirror_move(held_stash)
    out_local = forward(fwd_q[0], fwd_k[0], fwd_v[0], fwd_segments[0])
    fresh_stash = jnp.concatenate([fwd_q[0], fwd_k[0], fwd_v[0]], axis=1)
    fresh_stash = mirror_move(fresh_stash)
    arriving = shifted_2(up_grad[0], "section", -1)
    own_q = held_stash[:, :query_width]
    own_k = held_stash[:, query_width : query_width + key_width]
    own_v = held_stash[:, query_width + key_width :]
    grad_q, grad_k, grad_v = backward(own_q, own_k, own_v, back_segments[0], arriving)
    shifted = shifted_2(out_local, "section", 1)
    passed_output = lax.all_to_all(shifted, "tp", split_axis=0, concat_axis=1, tiled=True)
    evicted_q = fresh_stash[:, :query_width]
    evicted_k = fresh_stash[:, query_width : query_width + key_width]
    evicted_v = fresh_stash[:, query_width + key_width :]
    return (
        passed_output[None],
        evicted_q[None],
        evicted_k[None],
        evicted_v[None],
        grad_q[None],
        grad_k[None],
        grad_v[None],
    )


def solution(mesh):
    in_specs = (
        P("section", None, "tp"),
        P("section", None, "tp"),
        P("section", None, "tp"),
        P("section", None),
        P("section", None, "tp"),
        P("section", None, "tp"),
        P("section", None, "tp"),
        P("section", None),
        P("section", None, "tp"),
    )
    out_specs = (
        P("section", "tp", None),
        P("section", None, "tp"),
        P("section", None, "tp"),
        P("section", None, "tp"),
        P("section", None, "tp"),
        P("section", None, "tp"),
        P("section", None, "tp"),
    )
    return jax.shard_map(shards, mesh=mesh, in_specs=in_specs, out_specs=out_specs, check_vma=False)
```

profile of v0, /device:TPU:16, one launch (start us, length us, event | category | flops | bytes accessed | tf_op | source)
XLA Modules:
  0.0 199.5 jit_solution(10339786769427292944)
XLA Ops:
  0.7 1.5 copy.101
  2.5 2.3 %fusion.46 = (f32[4,8,128]{2,1,0:T(8,128)S(1)}, f32[4,8,128,128]{2,3,1,0:T(8,128)}) fusion(pred[128,128]{0,1:T(8,128)(4,1)S(1)} %fusion.32, bf16[128,4,8,128]{3,2,1,0:T(8,128)(2,1)S(1)} %bitcast.121, bf16[128,4,128,1]{2,1,0,3:T(4,128)(2,1)S(1)} %bitcast.131), kind=kOutput, calls=%fused_computation.51 | convolution fusion | flops 136315008 | bytes 3309568 | tf_op jit(solution)/shard_map/sub | solution.py:38
  4.7 2.0 %convolution_convert_fusion = bf16[4,8,128,128]{2,3,1,0:T(8,128)(2,1)S(1)} fusion(bf16[128,4,128,1]{0,2,3,1:T(8,128)(2,1)S(1)} %bitcast.123, f32[4,8,128,128]{2,3,1,0:T(8,128)} %get-tuple-element.33, f32[4,8,128]{2,1,0:T(8,128)S(1)} %get-tuple-element.32), kind=kOutput, calls=%fused_computation.15 | convolution fusion | flops 135790592 | bytes 3293184 | tf_op jit(solution)/shard_map/kgqs,skd->qkgd/dot_general | solution.py:46
  9.8 12.8 %collective-permute-done = bf16[128,4096]{1,0:T(8,128)(2,1)} collective-permute-done((bf16[128,4096]{1,0:T(8,128)(2,1)S(1)}, bf16[128,4096]{1,0:T(8,128)(2,1)}, u32[]{:S(2)}, u32[]{:S(2)}) %collective-permute-start) | collective-permute-done | bytes 1048608 | tf_op jit(solution)/shard_map/ppermute | solution.py:14
  22.6 4.4 %all-to-all-start = ((bf16[2,64,4096]{2,1,0:T(8,128)(2,1)}), bf16[2,64,4096]{2,1,0:T(8,128)(2,1)}, u32[]{:S(2)}, u32[]{:S(2)}) async-start(bf16[2,64,4096]{2,1,0:T(8,128)(2,1)} %bitcast.8), calls=%async_computation | async-start | bytes 2097152 | tf_op jit(solution)/shard_map/all_to_all | solution.py:98
  28.2 11.1 %all-to-all-done = bf16[2,64,4096]{2,1,0:T(8,128)(2,1)} async-done(((bf16[2,64,4096]{2,1,0:T(8,128)(2,1)}), bf16[2,64,4096]{2,1,0:T(8,128)(2,1)}, u32[]{:S(2)}, u32[]{:S(2)}) %all-to-all-start) | async-done | bytes 1048608 | tf_op jit(solution)/shard_map/all_to_all | solution.py:98
  39.3 5.4 %all-to-all-start.3 = ((bf16[128,16,320]{0,2,1:T(8,128)(2,1)}), bf16[128,16,320]{0,2,1:T(8,128)(2,1)S(1)}, u32[]{:S(2)}, u32[]{:S(2)}) async-start(bf16[128,16,320]{0,2,1:T(8,128)(2,1)} %bitcast.21), calls=%async_computation.3 | async-start | bytes 2621440 | tf_op jit(solution)/shard_map/all_to_all | solution.py:78
  46.1 2.4 %pad_maximum_fusion = bf16[128,5120]{0,1:T(8,128)(2,1)} fusion(bf16[128,512]{0,1:T(8,128)(2,1)S(1)} %bitcast.124, bf16[128,512]{0,1:T(8,128)(2,1)S(1)} %bitcast.127, bf16[128,4096]{0,1:T(8,128)(2,1)} %bitcast.116), kind=kLoop, calls=%fused_computation.17 | loop fusion | flops 3932160 | bytes 2621440 | tf_op jit(solution)/shard_map/concatenate | solution.py:90
  48.5 27.0 %all-to-all-done.3 = bf16[128,16,320]{0,2,1:T(8,128)(2,1)S(1)} async-done(((bf16[128,16,320]{0,2,1:T(8,128)(2,1)}), bf16[128,16,320]{0,2,1:T(8,128)(2,1)S(1)}, u32[]{:S(2)}, u32[]{:S(2)}) %all-to-all-start.3) | async-done | bytes 1310752 | tf_op jit(solution)/shard_map/all_to_all | solution.py:78
  75.4 4.6 %all-to-all-start.1 = ((bf16[128,16,320]{0,2,1:T(8,128)(2,1)}), bf16[128,16,320]{0,2,1:T(8,128)(2,1)S(1)}, u32[]{:S(2)}, u32[]{:S(2)}) async-start(bf16[128,16,320]{0,2,1:T(8,128)(2,1)} %bitcast.113), calls=%async_computation.1 | async-start | bytes 2621440 | tf_op jit(solution)/shard_map/all_to_all | solution.py:78
  81.3 29.6 %all-to-all-done.1 = bf16[128,16,320]{0,2,1:T(8,128)(2,1)S(1)} async-done(((bf16[128,16,320]{0,2,1:T(8,128)(2,1)}), bf16[128,16,320]{0,2,1:T(8,128)(2,1)S(1)}, u32[]{:S(2)}, u32[]{:S(2)}) %all-to-all-start.1) | async-done | bytes 1310752 | tf_op jit(solution)/shard_map/all_to_all | solution.py:78
  110.9 4.6 %all-to-all-start.4 = ((bf16[128,16,320]{0,2,1:T(8,128)(2,1)}), bf16[128,16,320]{0,2,1:T(8,128)(2,1)S(1)}, u32[]{:S(2)}, u32[]{:S(2)}) async-start(bf16[128,16,320]{0,2,1:T(8,128)(2,1)} %rev.8), calls=%async_computation.4 | async-start | bytes 2621440 | tf_op jit(solution)/shard_map/all_to_all | solution.py:80
  115.5 2.3 %copy.69 = bf16[1,128,4096]{1,2,0:T(8,128)(2,1)} copy(bf16[1,128,4096]{2,1,0:T(8,128)(2,1)} %param.17) | data formatting | bytes 2097152 | tf_op args[8]
  120.2 30.7 %all-to-all-done.4 = bf16[128,16,320]{0,2,1:T(8,128)(2,1)S(1)} async-done(((bf16[128,16,320]{0,2,1:T(8,128)(2,1)}), bf16[128,16,320]{0,2,1:T(8,128)(2,1)S(1)}, u32[]{:S(2)}, u32[]{:S(2)}) %all-to-all-start.4) | async-done | bytes 1310752 | tf_op jit(solution)/shard_map/all_to_all | solution.py:80
  150.9 11.3 %all-to-all-start.2 = ((bf16[128,16,320]{0,2,1:T(8,128)(2,1)}), bf16[128,16,320]{0,2,1:T(8,128)(2,1)S(1)}, u32[]{:S(2)}, u32[]{:S(2)}) async-start(bf16[128,16,320]{0,2,1:T(8,128)(2,1)} %rev.7), calls=%async_computation.2 | async-start | bytes 2621440 | tf_op jit(solution)/shard_map/all_to_all | solution.py:80
  162.3 3.3 %copy.60 = bf16[64,2,4096]{2,1,0:T(2,128)(2,1)} copy(bf16[64,2,4096]{2,0,1:T(8,128)(2,1)} %bitcast.9) | data formatting | bytes 2097152 | tf_op jit(solution)/shard_map/all_to_all | solution.py:98
  165.6 2.6 %broadcast_in_dim.38 = bf16[1,64,8192]{2,1,0:T(8,128)(2,1)} reshape(bf16[64,2,4096]{2,1,0:T(2,128)(2,1)} %copy.60) | data formatting | bytes 2097152 | tf_op jit(solution)/shard_map/broadcast_in_dim | solution.py:103
  169.3 1.7 fusion.52
  171.0 4.0 %fusion.51 = (f32[4,8,128]{2,1,0:T(8,128)}, f32[4,8,128,128]{2,3,1,0:T(8,128)}) fusion(pred[128,128]{0,1:T(8,128)(4,1)S(1)} %fusion.31, bf16[128,4,128,1]{0,2,3,1:T(8,128)(2,1)S(1)} %bitcast.132, bf16[128,4,8,128]{0,3,2,1:T(8,128)(2,1)} %bitcast.118), kind=kOutput, calls=%fused_computation.52 | convolution fusion | flops 136315008 | bytes 3309568 | tf_op jit(solution)/shard_map/sub | solution.py:38
  174.9 4.1 %convolution_convert_fusion.1 = bf16[4,128,8,128]{3,1,2,0:T(8,128)(2,1)} fusion(bf16[128,4,128,1]{0,2,3,1:T(8,128)(2,1)S(1)} %bitcast.133, f32[4,128,128,8]{2,1,3,0:T(8,128)S(1)} %fusion.52, f32[4,8,128,128]{2,3,1,0:T(8,128)} %get-tuple-element.35, f32[4,8,128]{2,1,0:T(8,128)} %get-tuple-element.34), kind=kOutput, calls=%fused_computation.16 | convolution fusion | flops 138416256 | bytes 5390336 | tf_op jit(solution)/shard_map/kgqs,skd->qkgd/dot_general | solution.py:64
  179.1 4.0 %fusion.8 = bf16[4,128,128]{2,1,0:T(8,128)(2,1)} fusion(bf16[128,4,8,128]{0,3,2,1:T(8,128)(2,1)} %bitcast.119, f32[4,128,128,8]{2,1,3,0:T(8,128)S(1)} %fusion.52, f32[4,8,128,128]{2,3,1,0:T(8,128)} %get-tuple-element.35, f32[4,8,128]{2,1,0:T(8,128)S(1)} %copy-done.12), kind=kOutput, calls=%fused_computation.21 | convolution fusion | flops 137957504 | bytes 5390336 | tf_op jit(solution)/shard_map/kgqs,qkgd->skd/dot_general | solution.py:65
  183.1 3.0 %fusion.9 = bf16[4,128,128]{1,2,0:T(8,128)(2,1)} fusion(bf16[128,4,8,128]{0,3,2,1:T(8,128)(2,1)} %bitcast.33, f32[4,8,128,128]{2,3,1,0:T(8,128)} %get-tuple-element.35, f32[4,8,128]{2,1,0:T(8,128)S(1)} %copy-done.12), kind=kOutput, calls=%fused_computation.22 | convolution fusion | flops 135331840 | bytes 3293184 | tf_op jit(solution)/shard_map/kgqs,qkgd->skd/dot_general | solution.py:56
  186.1 6.9 %all-to-all-done.2 = bf16[128,16,320]{0,2,1:T(8,128)(2,1)S(1)} async-done(((bf16[128,16,320]{0,2,1:T(8,128)(2,1)}), bf16[128,16,320]{0,2,1:T(8,128)(2,1)S(1)}, u32[]{:S(2)}, u32[]{:S(2)}) %all-to-all-start.2) | async-done | bytes 1310752 | tf_op jit(solution)/shard_map/all_to_all | solution.py:80
  193.8 1.3 copy.78
  (51 shorter events, 15.7 us)
Async XLA Ops:
  0.6 1.5 copy-start.3
  0.6 1.6 copy-start.10
  0.7 1.7 copy-start.6
  6.8 1.2 copy-start.1
  6.8 1.9 copy-start.7
  7.3 15.3 %collective-permute-start = (bf16[128,4096]{1,0:T(8,128)(2,1)S(1)}, bf16[128,4096]{1,0:T(8,128)(2,1)}, u32[]{:S(2)}, u32[]{:S(2)}) collective-permute-start(bf16[128,4096]{1,0:T(8,128)(2,1)S(1)} %copy.59), channel_id=1, source_target_pairs={{0,2},{2,4},{4,6},{6,8},{8,10},{10,12},{12,14},{14,16},{16,18},{18... | collective-permute-start | bytes 3145736 | tf_op jit(solution)/shard_map/ppermute | solution.py:14
  22.6 16.7 %all-to-all-start = ((bf16[2,64,4096]{2,1,0:T(8,128)(2,1)}), bf16[2,64,4096]{2,1,0:T(8,128)(2,1)}, u32[]{:S(2)}, u32[]{:S(2)}) async-start(bf16[2,64,4096]{2,1,0:T(8,128)(2,1)} %bitcast.8), calls=%async_computation | async-start | bytes 2097152 | tf_op jit(solution)/shard_map/all_to_all | solution.py:98
  27.0 17.6 %copy-start = (bf16[1,128,4096]{2,1,0:T(8,128)(2,1)S(1)}, bf16[1,128,4096]{2,1,0:T(8,128)(2,1)}, u32[]{:S(2)}) copy-start(bf16[1,128,4096]{2,1,0:T(8,128)(2,1)} %param.9) | copy-start | bytes 3145732
  39.3 6.7 %copy-start.4 = (bf16[1,128,512]{2,1,0:T(8,128)(2,1)S(1)}, bf16[1,128,512]{2,1,0:T(8,128)(2,1)}, u32[]{:S(2)}) copy-start(bf16[1,128,512]{2,1,0:T(8,128)(2,1)} %param.10) | copy-start | bytes 393220
  39.3 36.2 %all-to-all-start.3 = ((bf16[128,16,320]{0,2,1:T(8,128)(2,1)}), bf16[128,16,320]{0,2,1:T(8,128)(2,1)S(1)}, u32[]{:S(2)}, u32[]{:S(2)}) async-start(bf16[128,16,320]{0,2,1:T(8,128)(2,1)} %bitcast.21), calls=%async_computation.3 | async-start | bytes 2621440 | tf_op jit(solution)/shard_map/all_to_all | solution.py:78
  75.4 35.4 %all-to-all-start.1 = ((bf16[128,16,320]{0,2,1:T(8,128)(2,1)}), bf16[128,16,320]{0,2,1:T(8,128)(2,1)S(1)}, u32[]{:S(2)}, u32[]{:S(2)}) async-start(bf16[128,16,320]{0,2,1:T(8,128)(2,1)} %bitcast.113), calls=%async_computation.1 | async-start | bytes 2621440 | tf_op jit(solution)/shard_map/all_to_all | solution.py:78
  110.9 40.0 %all-to-all-start.4 = ((bf16[128,16,320]{0,2,1:T(8,128)(2,1)}), bf16[128,16,320]{0,2,1:T(8,128)(2,1)S(1)}, u32[]{:S(2)}, u32[]{:S(2)}) async-start(bf16[128,16,320]{0,2,1:T(8,128)(2,1)} %rev.8), calls=%async_computation.4 | async-start | bytes 2621440 | tf_op jit(solution)/shard_map/all_to_all | solution.py:80
  117.8 44.4 %copy-start.11 = (s32[1,128]{1,0:T(1,128)S(1)}, s32[1,128]{1,0:T(1,128)}, u32[]{:S(2)}) copy-start(s32[1,128]{1,0:T(1,128)} %param.16) | copy-start | bytes 1540
  117.8 51.5 %collective-permute-start.1 = (bf16[128,4096]{0,1:T(8,128)(2,1)}, bf16[128,4096]{0,1:T(8,128)(2,1)}, u32[]{:S(2)}, u32[]{:S(2)}) collective-permute-start(bf16[128,4096]{0,1:T(8,128)(2,1)} %bitcast.117), channel_id=1, source_target_pairs={{0,30},{2,0},{4,2},{6,4},{8,6},{10,8},{12,10},{14,12},{16,14},{18,... | collective-permute-start | bytes 3145736 | tf_op jit(solution)/shard_map/ppermute | solution.py:14
  150.9 42.1 %all-to-all-start.2 = ((bf16[128,16,320]{0,2,1:T(8,128)(2,1)}), bf16[128,16,320]{0,2,1:T(8,128)(2,1)S(1)}, u32[]{:S(2)}, u32[]{:S(2)}) async-start(bf16[128,16,320]{0,2,1:T(8,128)(2,1)} %rev.7), calls=%async_computation.2 | async-start | bytes 2621440 | tf_op jit(solution)/shard_map/all_to_all | solution.py:80
  174.9 4.1 %copy-start.12 = (f32[4,8,128]{2,1,0:T(8,128)S(1)}, f32[4,8,128]{2,1,0:T(8,128)}, u32[]{:S(2)}) copy-start(f32[4,8,128]{2,1,0:T(8,128)} %get-tuple-element.34) | copy-start | bytes 49156
  186.1 7.7 %copy-start.2 = (bf16[4,128,8,128]{3,1,2,0:T(8,128)(2,1)S(1)}, bf16[4,128,8,128]{3,1,2,0:T(8,128)(2,1)}, u32[]{:S(2)}) copy-start(bf16[4,128,8,128]{3,1,2,0:T(8,128)(2,1)} %convolution_convert_fusion.1) | copy-start | bytes 3145732
  193.7 1.4 copy-start.8
  193.7 2.1 %copy-start.9 = (bf16[4,128,128]{1,2,0:T(8,128)(2,1)S(1)}, bf16[4,128,128]{1,2,0:T(8,128)(2,1)}, u32[]{:S(2)}) copy-start(bf16[4,128,128]{1,2,0:T(8,128)(2,1)} %fusion.9) | copy-start | bytes 393220
  193.7 2.9 %copy-start.5 = (bf16[1,128,512]{1,2,0:T(8,128)(2,1)S(1)}, bf16[1,128,512]{1,2,0:T(8,128)(2,1)}, u32[]{:S(2)}) copy-start(bf16[1,128,512]{1,2,0:T(8,128)(2,1)} %get-tuple-element.31) | copy-start | bytes 393220
where the time goes:
time: 200 us; the launch traced here: 199 us
  waiting for transfers between devices  118 us (59%)
  starting transfers between devices  31.6 us (16%)
  local copies, waits for them, and re-layouts  24.1 us (12%)
  matrix products  21.1 us (11%)
  other arithmetic  3.71 us (2%)
    all_to_all x2, waiting for transfers between devices, mirror_move(): lax.all_to_all(pieces, 'section', split_axis=1, concat_axis=1, tiled=True)  56.6 us
    all_to_all x2, waiting for transfers between devices, mirror_move(): lax.all_to_all(flipped, 'section', split_axis=1, concat_axis=1, tiled=True)  37.7 us
    all_to_all x2, starting transfers between devices, mirror_move(): lax.all_to_all(flipped, 'section', split_axis=1, concat_axis=1, tiled=True)  15.9 us
    unnamed x39, local copies, waits for them, and re-layouts  13.3 us
    ppermute x2, waiting for transfers between devices, shifted_2(): return lax.ppermute(value, axis, pairs)  12.8 us
    all_to_all x1, waiting for transfers between devices, shards(): lax.all_to_all(shifted, 'tp', split_axis=0, concat_axis=1, tiled=True)  11.1 us
    all_to_all x2, starting transfers between devices, mirror_move(): lax.all_to_all(pieces, 'section', split_axis=1, concat_axis=1, tiled=True)  10 us
    sub x2, matrix products, probability(): weights = jnp.exp(scores - row_max)  6.24 us
  transfers between devices with their start and end apart: 7, of which 6 were waited for; matrix products, arithmetic and copies ran while one was open for 18% of the time, Pallas kernels for 0%

commit v1 on v0

--- a/solution.py
+++ b/solution.py
@@ -6,12 +6,6 @@
 HQ = 64
 KV = 8
 HD = 128
-
-
-def shifted_2(value, axis, steps):
-    count = lax.axis_size(axis)
-    pairs = [(source, (source + steps) % count) for source in range(count)]
-    return lax.ppermute(value, axis, pairs)
 
 
 def split_heads(queries, key_rows, value_rows):
@@ -70,35 +64,41 @@
     )
 
 
-def mirror_move(stash):
-    section_count = lax.axis_size("section")
-    row_count = stash.shape[0]
-    width = stash.shape[1]
-    pieces = stash.reshape(row_count, section_count, width // section_count)
-    spread = lax.all_to_all(pieces, "section", split_axis=1, concat_axis=1, tiled=True)
-    flipped = jnp.flip(spread, axis=1)
-    collected = lax.all_to_all(flipped, "section", split_axis=1, concat_axis=1, tiled=True)
-    return collected.reshape(row_count, width)
+def mirrored(value):
+    count = lax.axis_size("section")
+    return lax.ppermute(value, "section", [(j, count - 1 - j) for j in range(count)])
+
+
+def passed_on(out_local):
+    sections, splits = lax.axis_size("section"), lax.axis_size("tp")
+    own = lax.axis_index("tp")
+    rows, width = out_local.shape[0] // splits, out_local.shape[1]
+    passed = jnp.zeros((rows, splits, width), out_local.dtype)
+    for offset in range(splits):
+        piece = lax.dynamic_slice_in_dim(out_local, lax.rem(own + offset, splits) * rows, rows, 0)
+        pairs = [
+            (s * splits + t, (s + 1) % sections * splits + (t + offset) % splits)
+            for s in range(sections)
+            for t in range(splits)
+        ]
+        piece = lax.ppermute(piece, ("section", "tp"), pairs)
+        came_from = lax.rem(own - offset + splits, splits)
+        passed = lax.dynamic_update_slice_in_dim(passed, piece[:, None], came_from, 1)
+    return passed.reshape(rows, splits * width)
 
 
 def shards(fwd_q, fwd_k, fwd_v, fwd_segments, held_q, held_k, held_v, back_segments, up_grad):
-    query_width = fwd_q.shape[2]
-    key_width = fwd_k.shape[2]
-    held_stash = jnp.concatenate([held_q[0], held_k[0], held_v[0]], axis=1)
-    held_stash = mirror_move(held_stash)
+    sections = lax.axis_size("section")
+    own_k = mirrored(held_k[0])
+    own_q = mirrored(held_q[0])
+    own_v = mirrored(held_v[0])
+    arriving = lax.ppermute(up_grad[0], "section", [(j, (j - 1) % sections) for j in range(sections)])
     out_local = forward(fwd_q[0], fwd_k[0], fwd_v[0], fwd_segments[0])
-    fresh_stash = jnp.concatenate([fwd_q[0], fwd_k[0], fwd_v[0]], axis=1)
-    fresh_stash = mirror_move(fresh_stash)
-    arriving = shifted_2(up_grad[0], "section", -1)
-    own_q = held_stash[:, :query_width]
-    own_k = held_stash[:, query_width : query_width + key_width]
-    own_v = held_stash[:, query_width + key_width :]
+    passed_output = passed_on(out_local)
+    evicted_q = mirrored(fwd_q[0])
+    evicted_k = mirrored(fwd_k[0])
+    evicted_v = mirrored(fwd_v[0])
     grad_q, grad_k, grad_v = backward(own_q, own_k, own_v, back_segments[0], arriving)
-    shifted = shifted_2(out_local, "section", 1)
-    passed_output = lax.all_to_all(shifted, "tp", split_axis=0, concat_axis=1, tiled=True)
-    evicted_q = fresh_stash[:, :query_width]
-    evicted_k = fresh_stash[:, query_width : query_width + key_width]
-    evicted_v = fresh_stash[:, query_width + key_width :]
     return (
         passed_output[None],
         evicted_q[None],
@@ -111,24 +111,12 @@
 
 
 def solution(mesh):
-    in_specs = (
-        P("section", None, "tp"),
-        P("section", None, "tp"),
-        P("section", None, "tp"),
-        P("section", None),
-        P("section", None, "tp"),
-        P("section", None, "tp"),
-        P("section", None, "tp"),
-        P("section", None),
-        P("section", None, "tp"),
+    heads = P("section", None, "tp")
+    tokens = P("section", None)
+    return jax.shard_map(
+        shards,
+        mesh=mesh,
+        in_specs=(heads, heads, heads, tokens, heads, heads, heads, tokens, heads),
+        out_specs=(P("section", "tp", None),) + (heads,) * 6,
+        check_vma=False,
     )
-    out_specs = (
-        P("section", "tp", None),
-        P("section", None, "tp"),
-        P("section", None, "tp"),
-        P("section", None, "tp"),
-        P("section", None, "tp"),
-        P("section", None, "tp"),
-        P("section", None, "tp"),
-    )
-    return jax.shard_map(shards, mesh=mesh, in_specs=in_specs, out_specs=out_specs, check_vma=False)

time: 200 us -> 157 us (0.79)
  waiting for transfers between devices: 118 us -> 93.9 us
  starting transfers between devices: 31.6 us -> 8.27 us
  local copies, waits for them, and re-layouts: 24.1 us -> 33.7 us
  other arithmetic: 3.71 us -> 0.17 us
  matrix products: 21.1 us -> 18.2 us
    all_to_all x5 -> x0, waiting for transfers between devices: 105 us -> none  [the longest x2 56.6 us: mirror_move(): lax.all_to_all(pieces, 'section', split_axis=1, concat_axis=1, tiled=True)]
    ppermute x2 -> x9, waiting for transfers between devices: 12.8 us -> 93.9 us  [the longest x6 93.9 us: mirrored(): lax.ppermute(value, 'section', [(j, count - 1 - j) for j in range(count)])]
    all_to_all x5 -> x0, starting transfers between devices: 30.3 us -> none  [the longest x2 15.9 us: mirror_move(): lax.all_to_all(flipped, 'section', split_axis=1, concat_axis=1, tiled=True)]
    dynamic_update_slice x0 -> x2, local copies, waits for them, and re-layouts: none -> 13.3 us  [passed_on(): lax.dynamic_update_slice_in_dim(passed, piece[:, None], came_from, 1)]
    ppermute x2 -> x9, starting transfers between devices: 1.27 us -> 8.27 us  [the longest x6 5.64 us: mirrored(): lax.ppermute(value, 'section', [(j, count - 1 - j) for j in range(count)])]
    concatenate x2 -> x0, other arithmetic: 3.55 us -> none  [the longest x1 2.37 us: shards(): fresh_stash = jnp.concatenate([fwd_q[0], fwd_k[0], fwd_v[0]], axis=1)]
    all_to_all x1 -> x0, local copies, waits for them, and re-layouts: 3.29 us -> none  [shards(): lax.all_to_all(shifted, 'tp', split_axis=0, concat_axis=1, tiled=True)]
    rev x2 -> x0, local copies, waits for them, and re-layouts: 2.34 us -> none  [mirror_move(): flipped = jnp.flip(spread, axis=1)]
  transfers between devices with their start and end apart: 7 -> 9, of which waited for: 6 -> 2; matrix products, arithmetic and copies ran while one was open for 18% -> 28% of each run, Pallas kernels for 0% -> 0%
where the time goes in v1:
time: 157 us; the launch traced here: 155 us
  waiting for transfers between devices  93.9 us (60%)
  local copies, waits for them, and re-layouts  33.7 us (21%)
  matrix products  18.2 us (12%)
  starting transfers between devices  8.27 us (5%)
    ppermute x6, waiting for transfers between devices, mirrored(): lax.ppermute(value, 'section', [(j, count - 1 - j) for j in range(count)])  93.9 us
    unnamed x31, local copies, waits for them, and re-layouts  14.7 us
    dynamic_update_slice x2, local copies, waits for them, and re-layouts, passed_on(): lax.dynamic_update_slice_in_dim(passed, piece[:, None], came_from, 1)  13.3 us
    sub x2, matrix products, probability(): weights = jnp.exp(scores - row_max)  5.73 us
    ppermute x6, starting transfers between devices, mirrored(): lax.ppermute(value, 'section', [(j, count - 1 - j) for j in range(count)])  5.64 us
    dot_general x1, matrix products, backward(): jnp.einsum('kgqs,qkgd->skd', dscore, query_heads, preferred_element_type=...  3.3 us
    dot_general x1, matrix products, backward(): jnp.einsum('kgqs,skd->qkgd', dscore, key_heads, preferred_element_type=jn...  3.18 us
  transfers between devices with their start and end apart: 9, of which 2 were waited for; matrix products, arithmetic and copies ran while one was open for 28% of the time, Pallas kernels for 0%

profile of v1, /device:TPU:16, one launch (start us, length us, event | category | flops | bytes accessed | tf_op | source)
XLA Modules:
  0.0 155.2 jit_solution(13629425574199700119)
XLA Ops:
  0.7 2.4 %copy.64 = bf16[1,128,4096]{1,2,0:T(8,128)(2,1)} copy(bf16[1,128,4096]{2,1,0:T(8,128)(2,1)} %param.17) | data formatting | bytes 2097152 | tf_op args[8]
  3.9 1.3 copy.60
  6.1 1.4 copy.95
  7.6 2.3 %fusion.45 = (f32[4,8,128]{2,1,0:T(8,128)S(1)}, f32[4,8,128,128]{2,3,1,0:T(8,128)}) fusion(pred[128,128]{0,1:T(8,128)(4,1)S(1)} %fusion.32, bf16[128,4,8,128]{3,2,1,0:T(8,128)(2,1)S(1)} %bitcast.104, bf16[128,4,128,1]{2,1,0,3:T(4,128)(2,1)S(1)} %bitcast.115), kind=kOutput, calls=%fused_computation.47 | convolution fusion | flops 136315008 | bytes 3309568 | tf_op jit(solution)/shard_map/sub | solution.py:32
  9.8 2.0 %convolution_convert_fusion.1 = bf16[4,8,128,128]{2,3,1,0:T(8,128)(2,1)S(1)} fusion(bf16[128,4,128,1]{0,2,3,1:T(8,128)(2,1)S(1)} %bitcast.114, f32[4,8,128,128]{2,3,1,0:T(8,128)} %get-tuple-element.31, f32[4,8,128]{2,1,0:T(8,128)S(1)} %get-tuple-element.30), kind=kOutput, calls=%fused_computation.16 | convolution fusion | flops 135790592 | bytes 3293184 | tf_op jit(solution)/shard_map/kgqs,skd->qkgd/dot_general | solution.py:40
  13.0 1.1 copy.94
  14.1 1.8 %collective-permute-start.1 = (bf16[64,4096]{1,0:T(8,128)(2,1)}, bf16[64,4096]{1,0:T(8,128)(2,1)S(1)}, u32[]{:S(2)}, u32[]{:S(2)}) collective-permute-start(bf16[64,4096]{1,0:T(8,128)(2,1)} %copy.94), channel_id=1, source_target_pairs={{0,3},{1,2},{2,5},{3,4},{4,7},{5,6},{6,9},{7,8},{8,11},{9,10},{10,... | collective-permute-start | bytes 1572872 | tf_op jit(solution)/shard_map/ppermute | solution.py:84
  15.9 1.8 %collective-permute-start.4 = (bf16[128,512]{1,0:T(8,128)(2,1)S(1)}, bf16[128,512]{1,0:T(8,128)(2,1)S(1)}, u32[]{:S(2)}, u32[]{:S(2)}) collective-permute-start(bf16[128,512]{1,0:T(8,128)(2,1)S(1)} %bitcast.108), channel_id=1, source_target_pairs={{0,30},{2,28},{4,26},{6,24},{8,22},{10,20},{12,18},{14,16},{16,14}... | collective-permute-start | bytes 393224 | tf_op jit(solution)/shard_map/ppermute | solution.py:69
  17.7 88.6 %collective-permute-done.4 = bf16[128,512]{1,0:T(8,128)(2,1)S(1)} collective-permute-done((bf16[128,512]{1,0:T(8,128)(2,1)S(1)}, bf16[128,512]{1,0:T(8,128)(2,1)S(1)}, u32[]{:S(2)}, u32[]{:S(2)}) %collective-permute-start.4) | collective-permute-done | bytes 131104 | tf_op jit(solution)/shard_map/ppermute | solution.py:69
  107.9 5.2 %collective-permute-done.3 = bf16[128,512]{1,0:T(8,128)(2,1)S(1)} collective-permute-done((bf16[128,512]{1,0:T(8,128)(2,1)S(1)}, bf16[128,512]{1,0:T(8,128)(2,1)S(1)}, u32[]{:S(2)}, u32[]{:S(2)}) %collective-permute-start.3) | collective-permute-done | bytes 131104 | tf_op jit(solution)/shard_map/ppermute | solution.py:69
  113.8 2.2 %collective-permute-start.7 = (bf16[128,512]{0,1:T(8,128)(2,1)}, bf16[128,512]{0,1:T(8,128)(2,1)S(1)}, u32[]{:S(2)}, u32[]{:S(2)}) collective-permute-start(bf16[128,512]{0,1:T(8,128)(2,1)} %bitcast.24), channel_id=1, source_target_pairs={{0,30},{2,28},{4,26},{6,24},{8,22},{10,20},{12,18},{14,16},{16,14}... | collective-permute-start | bytes 393224 | tf_op jit(solution)/shard_map/ppermute | solution.py:69
  115.9 1.2 copy.56
  117.6 1.2 copy.58
  118.8 1.0 broadcast_in_dim.42
  119.8 6.6 %dynamic_update_slice.6 = bf16[64,2,4096]{2,1,0:T(2,128)(2,1)S(1)} dynamic-update-slice(bf16[64,2,4096]{2,1,0:T(2,128)(2,1)S(1)} %broadcast_in_dim.42, bf16[64,1,4096]{2,1,0:T(2,128)(2,1)S(1)} %copy.56, s32[]{:T(128)} %constant.27.clone.1, s32[]{:T(128)S(6)} %select_n.21, s32[]{:T(128)} %constant.27.clone.1) | dynamic-update-slice | bytes 1048580 | tf_op jit(solution)/shard_map/dynamic_update_slice | solution.py:86
  126.5 6.6 %dynamic_update_slice.7 = bf16[64,2,4096]{2,1,0:T(2,128)(2,1)S(1)} dynamic-update-slice(bf16[64,2,4096]{2,1,0:T(2,128)(2,1)S(1)} %dynamic_update_slice.6, bf16[64,1,4096]{2,1,0:T(2,128)(2,1)S(1)} %copy.58, s32[]{:T(128)} %constant.27.clone.1, s32[]{:T(128)S(6)} %select_n.23, s32[]{:T(128)} %constant.27.clone.1) | dynamic-update-slice | bytes 1048580 | tf_op jit(solution)/shard_map/dynamic_update_slice | solution.py:86
  133.1 1.6 %broadcast_in_dim_reshape.3 = bf16[1,64,8192]{2,1,0:T(8,128)(2,1)} reshape(bf16[64,2,4096]{2,1,0:T(2,128)(2,1)S(1)} %dynamic_update_slice.7) | data formatting | bytes 2097152 | tf_op jit(solution)/shard_map/broadcast_in_dim;reshape | solution.py:103
  134.7 3.4 %fusion.50 = (f32[4,8,128]{2,1,0:T(8,128)S(1)}, f32[4,8,128,128]{2,3,1,0:T(8,128)}) fusion(pred[128,128]{0,1:T(8,128)(4,1)S(1)} %fusion.31, bf16[128,4,128,1]{0,2,3,1:T(8,128)(2,1)} %bitcast.45, bf16[128,4,8,128]{0,3,2,1:T(8,128)(2,1)} %bitcast.22), kind=kOutput, calls=%fused_computation.48 | convolution fusion | flops 136315008 | bytes 3309568 | tf_op jit(solution)/shard_map/sub | solution.py:32
  138.2 1.7 %fusion.51 = f32[4,128,128,8]{2,1,3,0:T(8,128)S(1)} fusion(bf16[128,4,128,1]{0,2,3,1:T(8,128)(2,1)S(1)} %bitcast.107, bf16[128,4,8,128]{0,3,2,1:T(8,128)(2,1)} %bitcast.28), kind=kOutput, calls=%fused_computation.49 | convolution fusion | flops 134217728 | bytes 3276800 | tf_op jit(solution)/shard_map/qkgd,skd->kgqs/dot_general | solution.py:53
  139.9 3.3 %fusion.8 = bf16[4,128,128]{1,2,0:T(8,128)(2,1)S(1)} fusion(bf16[128,4,8,128]{0,3,2,1:T(8,128)(2,1)} %bitcast.22, f32[4,128,128,8]{2,1,3,0:T(8,128)S(1)} %fusion.51, f32[4,8,128,128]{2,3,1,0:T(8,128)} %get-tuple-element.33, f32[4,8,128]{2,1,0:T(8,128)S(1)} %get-tuple-element.32), kind=kOutput, calls=%fused_computation.19 | convolution fusion | flops 137957504 | bytes 5390336 | tf_op jit(solution)/shard_map/kgqs,qkgd->skd/dot_general | solution.py:59
  143.2 3.2 %convolution_convert_fusion = bf16[4,8,128,128]{2,3,1,0:T(8,128)(2,1)S(1)} fusion(bf16[128,4,128,1]{0,2,3,1:T(8,128)(2,1)} %bitcast.45, f32[4,128,128,8]{2,1,3,0:T(8,128)S(1)} %fusion.51, f32[4,8,128,128]{2,3,1,0:T(8,128)} %get-tuple-element.33, f32[4,8,128]{2,1,0:T(8,128)S(1)} %get-tuple-element.32), kind=kOutput, calls=%fused_computation.15 | convolution fusion | flops 138416256 | bytes 5390336 | tf_op jit(solution)/shard_map/kgqs,skd->qkgd/dot_general | solution.py:58
  146.4 2.3 %fusion.9 = bf16[4,128,128]{1,2,0:T(8,128)(2,1)S(1)} fusion(bf16[128,4,8,128]{0,3,2,1:T(8,128)(2,1)} %bitcast.28, f32[4,8,128,128]{2,3,1,0:T(8,128)} %get-tuple-element.33, f32[4,8,128]{2,1,0:T(8,128)S(1)} %get-tuple-element.32), kind=kOutput, calls=%fused_computation.20 | convolution fusion | flops 135331840 | bytes 3293184 | tf_op jit(solution)/shard_map/kgqs,qkgd->skd/dot_general | solution.py:50
  148.7 1.3 copy.70
  151.6 2.3 %copy.121 = bf16[1,128,4096]{2,1,0:T(8,128)(2,1)} copy(bf16[1,128,4096]{2,1,0:T(8,128)(2,1)} %bitcast.12) | data formatting | bytes 2097152
  (43 shorter events, 8.4 us)
Async XLA Ops:
  0.6 3.2 %copy-start = (bf16[1,128,4096]{2,1,0:T(8,128)(2,1)S(1)}, bf16[1,128,4096]{2,1,0:T(8,128)(2,1)}, u32[]{:S(2)}) copy-start(bf16[1,128,4096]{2,1,0:T(8,128)(2,1)} %param.13) | copy-start | bytes 3145732
  0.6 5.2 %copy-start.7 = (s32[1,128]{1,0:T(1,128)S(1)}, s32[1,128]{1,0:T(1,128)}, u32[]{:S(2)}) copy-start(s32[1,128]{1,0:T(1,128)} %param.12) | copy-start | bytes 1540
  0.7 5.3 %copy-start.4 = (bf16[1,128,512]{2,1,0:T(8,128)(2,1)S(1)}, bf16[1,128,512]{2,1,0:T(8,128)(2,1)}, u32[]{:S(2)}) copy-start(bf16[1,128,512]{2,1,0:T(8,128)(2,1)} %param.10) | copy-start | bytes 393220
  0.7 5.3 %copy-start.1 = (bf16[1,128,512]{2,1,0:T(8,128)(2,1)S(1)}, bf16[1,128,512]{2,1,0:T(8,128)(2,1)}, u32[]{:S(2)}) copy-start(bf16[1,128,512]{2,1,0:T(8,128)(2,1)} %param.11) | copy-start | bytes 393220
  3.0 135.1 %collective-permute-start.8 = (bf16[128,4096]{0,1:T(8,128)(2,1)}, bf16[128,4096]{0,1:T(8,128)(2,1)}, u32[]{:S(2)}, u32[]{:S(2)}) collective-permute-start(bf16[128,4096]{0,1:T(8,128)(2,1)} %bitcast.27), channel_id=1, source_target_pairs={{0,30},{2,0},{4,2},{6,4},{8,6},{10,8},{12,10},{14,12},{16,14},{18,... | collective-permute-start | bytes 3145736 | tf_op jit(solution)/shard_map/ppermute | solution.py:95
  5.2 129.6 %collective-permute-start.6 = (bf16[128,4096]{0,1:T(8,128)(2,1)}, bf16[128,4096]{0,1:T(8,128)(2,1)}, u32[]{:S(2)}, u32[]{:S(2)}) collective-permute-start(bf16[128,4096]{0,1:T(8,128)(2,1)} %bitcast.21), channel_id=1, source_target_pairs={{0,30},{2,28},{4,26},{6,24},{8,22},{10,20},{12,18},{14,16},{16,14}... | collective-permute-start | bytes 3145736 | tf_op jit(solution)/shard_map/ppermute | solution.py:69
  12.5 93.8 %copy-start.2 = (bf16[1,128,512]{2,1,0:T(8,128)(2,1)S(1)}, bf16[1,128,512]{2,1,0:T(8,128)(2,1)}, u32[]{:S(2)}) copy-start(bf16[1,128,512]{2,1,0:T(8,128)(2,1)} %param.14) | copy-start | bytes 393220
  12.5 94.6 %copy-start.3 = (bf16[1,128,512]{2,1,0:T(8,128)(2,1)S(1)}, bf16[1,128,512]{2,1,0:T(8,128)(2,1)}, u32[]{:S(2)}) copy-start(bf16[1,128,512]{2,1,0:T(8,128)(2,1)} %param.15) | copy-start | bytes 393220
  12.6 101.0 %copy-start.8 = (s32[1,128]{1,0:T(1,128)S(1)}, s32[1,128]{1,0:T(1,128)}, u32[]{:S(2)}) copy-start(s32[1,128]{1,0:T(1,128)} %param.16) | copy-start | bytes 1540
  12.9 100.7 %collective-permute-start = (bf16[64,4096]{1,0:T(8,128)(2,1)S(1)}, bf16[64,4096]{1,0:T(8,128)(2,1)S(1)}, u32[]{:S(2)}, u32[]{:S(2)}) collective-permute-start(bf16[64,4096]{1,0:T(8,128)(2,1)S(1)} %copy.93), channel_id=1, source_target_pairs={{0,2},{1,3},{2,4},{3,5},{4,6},{5,7},{6,8},{7,9},{8,10},{9,11},{10,... | collective-permute-start | bytes 1572872 | tf_op jit(solution)/shard_map/ppermute | solution.py:84
  14.1 103.0 %collective-permute-start.1 = (bf16[64,4096]{1,0:T(8,128)(2,1)}, bf16[64,4096]{1,0:T(8,128)(2,1)S(1)}, u32[]{:S(2)}, u32[]{:S(2)}) collective-permute-start(bf16[64,4096]{1,0:T(8,128)(2,1)} %copy.94), channel_id=1, source_target_pairs={{0,3},{1,2},{2,5},{3,4},{4,7},{5,6},{6,9},{7,8},{8,11},{9,10},{10,... | collective-permute-start | bytes 1572872 | tf_op jit(solution)/shard_map/ppermute | solution.py:84
  15.9 90.5 %collective-permute-start.4 = (bf16[128,512]{1,0:T(8,128)(2,1)S(1)}, bf16[128,512]{1,0:T(8,128)(2,1)S(1)}, u32[]{:S(2)}, u32[]{:S(2)}) collective-permute-start(bf16[128,512]{1,0:T(8,128)(2,1)S(1)} %bitcast.108), channel_id=1, source_target_pairs={{0,30},{2,28},{4,26},{6,24},{8,22},{10,20},{12,18},{14,16},{16,14}... | collective-permute-start | bytes 393224 | tf_op jit(solution)/shard_map/ppermute | solution.py:69
  106.3 6.8 %collective-permute-start.3 = (bf16[128,512]{1,0:T(8,128)(2,1)S(1)}, bf16[128,512]{1,0:T(8,128)(2,1)S(1)}, u32[]{:S(2)}, u32[]{:S(2)}) collective-permute-start(bf16[128,512]{1,0:T(8,128)(2,1)S(1)} %bitcast.109), channel_id=1, source_target_pairs={{0,30},{2,28},{4,26},{6,24},{8,22},{10,20},{12,18},{14,16},{16,14}... | collective-permute-start | bytes 393224 | tf_op jit(solution)/shard_map/ppermute | solution.py:69
  113.1 0.7 copy-start.5
  113.1 21.6 %collective-permute-start.5 = (bf16[128,512]{0,1:T(8,128)(2,1)}, bf16[128,512]{0,1:T(8,128)(2,1)}, u32[]{:S(2)}, u32[]{:S(2)}) collective-permute-start(bf16[128,512]{0,1:T(8,128)(2,1)} %bitcast.18), channel_id=1, source_target_pairs={{0,30},{2,28},{4,26},{6,24},{8,22},{10,20},{12,18},{14,16},{16,14}... | collective-permute-start | bytes 393224 | tf_op jit(solution)/shard_map/ppermute | solution.py:69
  113.8 24.4 %collective-permute-start.7 = (bf16[128,512]{0,1:T(8,128)(2,1)}, bf16[128,512]{0,1:T(8,128)(2,1)S(1)}, u32[]{:S(2)}, u32[]{:S(2)}) collective-permute-start(bf16[128,512]{0,1:T(8,128)(2,1)} %bitcast.24), channel_id=1, source_target_pairs={{0,30},{2,28},{4,26},{6,24},{8,22},{10,20},{12,18},{14,16},{16,14}... | collective-permute-start | bytes 393224 | tf_op jit(solution)/shard_map/ppermute | solution.py:69
  117.1 31.6 %collective-permute-start.2 = (bf16[128,4096]{1,0:T(8,128)(2,1)}, bf16[128,4096]{1,0:T(8,128)(2,1)}, u32[]{:S(2)}, u32[]{:S(2)}) collective-permute-start(bf16[128,4096]{1,0:T(8,128)(2,1)} %bitcast.11), channel_id=1, source_target_pairs={{0,30},{2,28},{4,26},{6,24},{8,22},{10,20},{12,18},{14,16},{16,14}... | collective-permute-start | bytes 3145736 | tf_op jit(solution)/shard_map/ppermute | solution.py:69
  148.7 5.2 %copy-start.6 = (bf16[128,512]{1,0:T(8,128)(2,1)S(1)}, bf16[128,512]{1,0:T(8,128)(2,1)}, u32[]{:S(2)}) copy-start(bf16[128,512]{1,0:T(8,128)(2,1)} %copy-done.5) | copy-start | bytes 393220

commit v2 on v1

v2 whole, which is shorter than its diff:
```python
import functools

import jax
import jax.numpy as jnp
from jax import lax
from jax.experimental import pallas as pl
from jax.experimental.pallas import tpu as pltpu
from jax.sharding import PartitionSpec as P

HQ = 64
KV = 8
HD = 128
GROUP = HQ // KV
SCALE = HD**-0.5
LOW = jnp.bfloat16
F32 = jnp.float32
DIAG_ROWS = 16


def dot_nt(a, b):
    return lax.dot_general(a, b, (((1,), (1,)), ((), ())), preferred_element_type=F32)


def dot_tn(a, b):
    return lax.dot_general(a, b, (((0,), (0,)), ((), ())), preferred_element_type=F32)


def dot_nn(a, b):
    return lax.dot_general(a, b, (((1,), (0,)), ((), ())), preferred_element_type=F32)


def iotas(shape):
    return lax.broadcasted_iota(jnp.int32, shape, 0), lax.broadcasted_iota(jnp.int32, shape, 1)


def allowed_mask(seg_col, seg_row):
    tokens = seg_row.shape[1]
    rows, cols = iotas((tokens, tokens))
    return (seg_col == seg_row) & (cols <= rows)


def probability(q, k, allowed):
    scores = jnp.where(allowed, dot_nt(q, k) * SCALE, -jnp.inf)
    weights = jnp.exp(scores - jnp.max(scores, axis=1, keepdims=True))
    return weights / jnp.sum(weights, axis=1, keepdims=True)


def pack(full):
    half = full.shape[0] // 2
    rows, cols = iotas((half, half))
    turned = full[half:, :].T
    packed = full[:half, :half] + turned[:half] + jnp.where(rows < cols, turned[half:], 0.0)
    diag = jnp.sum(jnp.where(rows == cols, full[half:, half:], 0.0), axis=0, keepdims=True)
    return packed, diag


def unpack_masks(seg_col, seg_row):
    half = seg_row.shape[1] // 2
    rows, cols = iotas((half, half))
    first = (seg_col[:half] == seg_row[:, :half]) & (cols <= rows)
    cross = seg_col[:half] == seg_row[:, half:]
    second = (seg_col[half:] == seg_row[:, half:]) & (rows < cols)
    return first, jnp.concatenate([cross, second], axis=0), rows == cols


def unpack(packed, diag, masks):
    first, turned_mask, eye = masks
    turned = jnp.where(turned_mask, jnp.concatenate([packed, packed], axis=0), 0.0).T
    half = packed.shape[0]
    zero = jnp.zeros((half, half), F32)
    on_diag = jnp.where(eye, jnp.broadcast_to(diag, (half, half)), 0.0)
    top = jnp.concatenate([jnp.where(first, packed, 0.0), zero], axis=1)
    bottom = turned + jnp.concatenate([zero, on_diag], axis=1)
    return jnp.concatenate([top, bottom], axis=0)


def store_packed(g, kv_local, parts, diag_scratch, pack_ref):
    half = parts[0][0].shape[0]
    values = jnp.concatenate([p for p, _ in parts], axis=1).astype(LOW)
    pack_ref[pl.ds(pl.multiple_of(g * half, half), half), :] = values
    diags = jnp.concatenate([d for _, d in parts], axis=1)
    rows, _ = iotas(diag_scratch.shape)
    merged = jnp.where(rows == g, jnp.broadcast_to(diags, rows.shape), diag_scratch[...])
    diag_scratch[...] = merged

    @pl.when(g == kv_local - 1)
    def _():
        pack_ref[pl.ds(kv_local * half, DIAG_ROWS), :] = jnp.where(rows < kv_local, merged, 0.0).astype(LOW)


def load_packed(g, kv_local, pack_ref):
    half = (pack_ref.shape[0] - DIAG_ROWS) // kv_local
    values = pack_ref[pl.ds(pl.multiple_of(g * half, half), half), :].astype(F32)
    tail = pack_ref[pl.ds(kv_local * half, DIAG_ROWS), :].astype(F32)
    rows, _ = iotas(tail.shape)
    diags = jnp.sum(jnp.where(rows == g, tail, 0.0), axis=0, keepdims=True)
    return [
        (values[:, h * half : (h + 1) * half], diags[:, h * half : (h + 1) * half]) for h in range(GROUP)
    ]


def head(h):
    return slice(h * HD, (h + 1) * HD)


def forward_body(q_ref, k_ref, v_ref, seg_col, seg_row, out_ref):
    allowed = allowed_mask(seg_col[...], seg_row[...])
    k, v = k_ref[...], v_ref[...]
    for h in range(GROUP):
        prob = probability(q_ref[:, head(h)], k, allowed)
        out_ref[:, head(h)] = dot_nn(prob.astype(LOW), v).astype(LOW)


def score_gradient(prob, grad, v):
    dprob = dot_nt(grad, v)
    delta = jnp.sum(prob * dprob, axis=1, keepdims=True)
    return prob * (dprob - delta) * SCALE


def holder_body(kv_local, special, q_ref, k_ref, v_ref, grad_ref, seg_col, seg_row, pack_ref, third_ref, diag_scratch):
    g = pl.program_id(0)
    allowed = allowed_mask(seg_col[...], seg_row[...])
    k = k_ref[...]

    @pl.when(special[0] == 0)
    def _():
        parts = [pack(probability(q_ref[:, head(h)], k, allowed)) for h in range(GROUP)]
        store_packed(g, kv_local, parts, diag_scratch, pack_ref)
        third_ref[...] = v_ref[...]

    @pl.when(special[0] != 0)
    def _():
        v = v_ref[...]
        parts = []
        total = jnp.zeros(third_ref.shape, F32)
        for h in range(GROUP):
            prob = probability(q_ref[:, head(h)], k, allowed)
            grad = grad_ref[:, head(h)]
            total = total + dot_tn(prob.astype(LOW), grad)
            parts.append(pack(score_gradient(prob, grad, v)))
        store_packed(g, kv_local, parts, diag_scratch, pack_ref)
        third_ref[...] = total.astype(LOW)


def section_body(kv_local, special, in_ref, k_ref, third_ref, grad_ref, seg_col, seg_row, pack_ref, gq_ref, gv_ref, diag_scratch):
    g = pl.program_id(0)
    masks = unpack_masks(seg_col[...], seg_row[...])
    k = k_ref[...]

    @pl.when(special[0] == 0)
    def _():
        v = third_ref[...]
        parts = []
        total = jnp.zeros(gv_ref.shape, F32)
        for h, (packed, diag) in enumerate(load_packed(g, kv_local, in_ref)):
            prob = unpack(packed, diag, masks)
            grad = grad_ref[:, head(h)]
            total = total + dot_tn(prob.astype(LOW), grad)
            dscore = score_gradient(prob, grad, v)
            gq_ref[:, head(h)] = dot_nn(dscore.astype(LOW), k).astype(LOW)
            parts.append(pack(dscore))
        store_packed(g, kv_local, parts, diag_scratch, pack_ref)
        gv_ref[...] = total.astype(LOW)

    @pl.when(special[0] != 0)
    def _():
        pack_ref[...] = in_ref[...]
        gv_ref[...] = third_ref[...]
        for h, (packed, diag) in enumerate(load_packed(g, kv_local, in_ref)):
            dscore = unpack(packed, diag, masks)
            gq_ref[:, head(h)] = dot_nn(dscore.astype(LOW), k).astype(LOW)


def key_body(kv_local, pack_ref, q_ref, seg_col, seg_row, gk_ref):
    g = pl.program_id(0)
    masks = unpack_masks(seg_col[...], seg_row[...])
    total = jnp.zeros(gk_ref.shape, F32)
    for h, (packed, diag) in enumerate(load_packed(g, kv_local, pack_ref)):
        dscore = unpack(packed, diag, masks).astype(LOW)
        total = total + dot_tn(dscore, q_ref[:, head(h)])
    gk_ref[...] = total.astype(LOW)


def specs(tokens):
    wide = pl.BlockSpec((tokens, GROUP * HD), lambda g: (0, g))
    narrow = pl.BlockSpec((tokens, HD), lambda g: (0, g))
    seg = [pl.BlockSpec((tokens, 1), lambda g: (0, 0)), pl.BlockSpec((1, tokens), lambda g: (0, 0))]
    return wide, narrow, seg


def run(body, kv_local, in_specs, out_specs, out_shape, scratch, gflop, args):
    return pl.pallas_call(
        body,
        grid=(kv_local,),
        in_specs=in_specs,
        out_specs=out_specs,
        out_shape=out_shape,
        scratch_shapes=scratch,
        compiler_params=pltpu.CompilerParams(vmem_limit_bytes=24 * 2**20),
        cost_estimate=pl.CostEstimate(flops=int(gflop * 2**30), bytes_accessed=2**22, transcendentals=0),
    )(*args)


def mirrored(value):
    count = lax.axis_size("section")
    return lax.ppermute(value, "section", [(j, count - 1 - j) for j in range(count)])


def passed_on(out_local):
    sections, splits = lax.axis_size("section"), lax.axis_size("tp")
    own = lax.axis_index("tp")
    rows, width = out_local.shape[0] // splits, out_local.shape[1]
    came = []
    for offset in range(splits):
        piece = lax.dynamic_slice_in_dim(out_local, lax.rem(own + offset, splits) * rows, rows, 0)
        pairs = [
            (s * splits + t, (s + 1) % sections * splits + (t + offset) % splits)
            for s in range(sections)
            for t in range(splits)
        ]
        came.append(lax.ppermute(piece, ("section", "tp"), pairs))
    blocks = []
    for place in range(splits):
        offset = lax.rem(own - place + splits, splits)
        blocks.append(lax.select_n(offset, *came) if splits > 2 else jnp.where(offset == 0, came[0], came[-1]))
    return jnp.concatenate(blocks, axis=1)


def shards(fwd_q, fwd_k, fwd_v, fwd_segments, held_q, held_k, held_v, back_segments, up_grad):
    sections = lax.axis_size("section")
    me = lax.axis_index("section")
    tokens, half = held_q.shape[1], held_q.shape[1] // 2
    kv_local = held_k.shape[2] // HD
    wide, narrow, seg = specs(tokens)
    smem = pl.BlockSpec(memory_space=pltpu.SMEM)
    pack_shape = (kv_local * half + DIAG_ROWS, GROUP * half)
    whole = pl.BlockSpec(pack_shape, lambda g: (0, 0))
    packed_type = jax.ShapeDtypeStruct(pack_shape, LOW)
    wide_type = jax.ShapeDtypeStruct(held_q.shape[1:], LOW)
    narrow_type = jax.ShapeDtypeStruct(held_k.shape[1:], LOW)
    diag_scratch = [pltpu.VMEM((DIAG_ROWS, GROUP * half), F32)]

    def columns(ids):
        return ids.reshape(tokens, 1), ids.reshape(1, tokens)

    shortcuts = [i for i in range(sections) if (i + 1) % sections == sections - 1 - i]
    section_special = sum([(me == i).astype(jnp.int32) for i in shortcuts]).reshape(1)
    holder_special = sum([(me == sections - 1 - i).astype(jnp.int32) for i in shortcuts]).reshape(1)

    held_ids = mirrored(back_segments[0])
    evicted_k = mirrored(fwd_k[0])
    evicted_v = mirrored(fwd_v[0])
    evicted_q = mirrored(fwd_q[0])
    keys = mirrored(held_k[0])
    arriving = lax.ppermute(
        up_grad[0],
        "section",
        [((i + 1) % sections, i) for i in range(sections) if i not in shortcuts],
    )
    packed, third = run(
        functools.partial(holder_body, kv_local),
        kv_local,
        [smem, wide, narrow, narrow, wide] + seg,
        [whole, narrow],
        [packed_type, narrow_type],
        diag_scratch,
        0.3,
        (holder_special, held_q[0], held_k[0], held_v[0], up_grad[0]) + columns(held_ids),
    )
    packed_here, third_here = mirrored(packed), mirrored(third)
    out_local = run(
        forward_body,
        kv_local,
        [wide, narrow, narrow] + seg,
        wide,
        wide_type,
        [],
        0.3,
        (fwd_q[0], fwd_k[0], fwd_v[0]) + columns(fwd_segments[0]),
    )
    passed_output = passed_on(out_local)
    dscore, grad_q, grad_v = run(
        functools.partial(section_body, kv_local),
        kv_local,
        [smem, whole, narrow, narrow, wide] + seg,
        [whole, wide, narrow],
        [packed_type, wide_type, narrow_type],
        diag_scratch,
        0.5,
        (section_special, packed_here, keys, third_here, arriving) + columns(back_segments[0]),
    )
    dscore_back = lax.ppermute(
        dscore, "section", [(i, sections - 1 - i) for i in range(sections) if i not in shortcuts]
    )
    dscore_held = jnp.where(holder_special[0] != 0, packed, dscore_back)
    grad_k = run(
        functools.partial(key_body, kv_local),
        kv_local,
        [whole, wide] + seg,
        narrow,
        narrow_type,
        [],
        0.2,
        (dscore_held, held_q[0]) + columns(held_ids),
    )
    grad_k = mirrored(grad_k)
    return (
        passed_output[None],
        evicted_q[None],
        evicted_k[None],
        evicted_v[None],
        grad_q[None],
        grad_k[None],
        grad_v[None],
    )


def solution(mesh):
    heads = P("section", None, "tp")
    tokens = P("section", None)
    return jax.shard_map(
        shards,
        mesh=mesh,
        in_specs=(heads, heads, heads, tokens, heads, heads, heads, tokens, heads),
        out_specs=(P("section", "tp", None),) + (heads,) * 6,
        check_vma=False,
    )
```

time: 157 us -> 158 us (level)
  the two profiles are of different devices: /device:TPU:16 before, /device:TPU:23 now
where the time goes in v2:
time: 158 us; the launch traced here: 157 us
  waiting for transfers between devices  90 us (57%)
  Pallas kernels  36 us (23%)
  starting transfers between devices  18.4 us (12%)
  local copies, waits for them, and re-layouts  9.6 us (6%)
  other arithmetic  2.36 us (1%)
    ppermute x8, waiting for transfers between devices, mirrored(): lax.ppermute(value, 'section', [(j, count - 1 - j) for j in range(count)])  75.9 us
    pallas_call x4, Pallas kernels, run(): pl.pallas_call(body, grid=(kv_local,), in_specs=in_specs, out_specs=out_s...  36 us
    ppermute x1, waiting for transfers between devices, shards(): lax.ppermute(dscore, 'section', [(i, sections - 1 - i) for i in range(sec...  14.2 us
    ppermute x8, starting transfers between devices, mirrored(): lax.ppermute(value, 'section', [(j, count - 1 - j) for j in range(count)])  9.32 us
    unnamed x22, local copies, waits for them, and re-layouts  7.55 us
    ppermute x1, starting transfers between devices, shards(): lax.ppermute(dscore, 'section', [(i, sections - 1 - i) for i in range(sec...  4.55 us
  transfers between devices with their start and end apart: 12, of which 5 were waited for; matrix products, arithmetic and copies ran while one was open for 3% of the time, Pallas kernels for 23%

profile of v2, /device:TPU:23, one launch (start us, length us, event | category | flops | bytes accessed | tf_op | source)
XLA Modules:
  0.0 157.3 jit_solution(9867999636191926183)
XLA Ops:
  0.6 2.6 %collective-permute-start.9 = (bf16[128,4096]{1,0:T(8,128)(2,1)}, bf16[128,4096]{1,0:T(8,128)(2,1)}, u32[]{:S(2)}, u32[]{:S(2)}) collective-permute-start(bf16[128,4096]{1,0:T(8,128)(2,1)} %bitcast.24), channel_id=1, source_target_pairs={{2,0},{4,2},{6,4},{8,6},{10,8},{12,10},{14,12},{18,16},{20,18},{22... | collective-permute-start | bytes 3145736 | tf_op jit(solution)/shard_map/ppermute | solution.py:255
  3.2 0.8 copy.16.seg_col
  4.0 1.2 copy-done.2
  5.2 0.9 copy-done.5
  6.8 11.7 %shard_map.144 = bf16[128,4096]{1,0:T(8,128)(2,1)S(1)} custom-call(bf16[128,4096]{1,0:T(8,128)(2,1)S(1)} %bitcast.26, bf16[128,512]{1,0:T(8,128)(2,1)} %bitcast.1.k_ref, bf16[128,512]{1,0:T(8,128)(2,1)S(1)} %bitcast.29, s32[128,1]{1,0:T(8,128)S(1)} %copy.16.seg_col, s32[1,128]{1,0:T(1,128)S(1)} %copy-done.7), custom_call_target="tpu_custom_call" | custom-call | flops 322122560 | bytes 4194304 | tf_op jit(solution)/shard_map/pallas_call | solution.py:192
  18.5 1.1 constant_dynamic-slice_fusion
  19.6 2.0 %collective-permute-start = (bf16[64,4096]{1,0:T(8,128)(2,1)}, bf16[64,4096]{1,0:T(8,128)(2,1)}, u32[]{:S(2)}, u32[]{:S(2)}) collective-permute-start(bf16[64,4096]{1,0:T(8,128)(2,1)} %get-tuple-element.20), channel_id=1, source_target_pairs={{0,2},{1,3},{2,4},{3,5},{4,6},{5,7},{6,8},{7,9},{8,10},{9,11},{10,... | collective-permute-start | bytes 1572872 | tf_op jit(solution)/shard_map/ppermute | solution.py:221
  21.5 2.6 %collective-permute-start.5 = (s32[128]{0:T(128)S(1)}, s32[128]{0:T(128)S(1)}, u32[]{:S(2)}, u32[]{:S(2)}) collective-permute-start(s32[128]{0:T(128)S(1)} %bitcast.35), channel_id=1, source_target_pairs={{0,30},{2,28},{4,26},{6,24},{8,22},{10,20},{12,18},{14,16},{16,14}... | collective-permute-start | bytes 1544 | tf_op jit(solution)/shard_map/ppermute | solution.py:206
  24.2 16.3 %collective-permute-done.5 = s32[128]{0:T(128)S(1)} collective-permute-done((s32[128]{0:T(128)S(1)}, s32[128]{0:T(128)S(1)}, u32[]{:S(2)}, u32[]{:S(2)}) %collective-permute-start.5) | collective-permute-done | bytes 544 | tf_op jit(solution)/shard_map/ppermute | solution.py:206
  40.5 3.4 %collective-permute-start.3 = (bf16[128,512]{1,0:T(8,128)(2,1)}, bf16[128,512]{1,0:T(8,128)(2,1)}, u32[]{:S(2)}, u32[]{:S(2)}) collective-permute-start(bf16[128,512]{1,0:T(8,128)(2,1)} %bitcast.1.k_ref), channel_id=1, source_target_pairs={{0,30},{2,28},{4,26},{6,24},{8,22},{10,20},{12,18},{14,16},{16,14}... | collective-permute-start | bytes 393224 | tf_op jit(solution)/shard_map/ppermute | solution.py:206
  44.0 0.9 copy-done.4
  44.9 7.7 %shard_map.145 = (bf16[272,512]{1,0:T(8,128)(2,1)S(1)}, bf16[128,512]{1,0:T(8,128)(2,1)}) custom-call(s32[1]{0:T(128)} %bitcast.9.special, bf16[128,4096]{1,0:T(8,128)(2,1)S(1)} %bitcast.22, bf16[128,512]{1,0:T(8,128)(2,1)} %bitcast.11.k_ref, bf16[128,512]{1,0:T(8,128)(2,1)S(1)} %bitcast.28, bf16[128,4096]{1,0:T(8,128)(2,1)S(1)} %bitcast.25, ...), custom_call_target="tpu_custom_call" | custom-call | flops 322122560 | bytes 4194304 | tf_op jit(solution)/shard_map/pallas_call | solution.py:192
  52.7 3.2 %collective-permute-start.4 = (bf16[128,512]{1,0:T(8,128)(2,1)S(1)}, bf16[128,512]{1,0:T(8,128)(2,1)S(1)}, u32[]{:S(2)}, u32[]{:S(2)}) collective-permute-start(bf16[128,512]{1,0:T(8,128)(2,1)S(1)} %bitcast.30), channel_id=1, source_target_pairs={{0,30},{2,28},{4,26},{6,24},{8,22},{10,20},{12,18},{14,16},{16,14}... | collective-permute-start | bytes 393224 | tf_op jit(solution)/shard_map/ppermute | solution.py:206
  55.9 46.2 %collective-permute-done.4 = bf16[128,512]{1,0:T(8,128)(2,1)S(1)} collective-permute-done((bf16[128,512]{1,0:T(8,128)(2,1)S(1)}, bf16[128,512]{1,0:T(8,128)(2,1)S(1)}, u32[]{:S(2)}, u32[]{:S(2)}) %collective-permute-start.4) | collective-permute-done | bytes 131104 | tf_op jit(solution)/shard_map/ppermute | solution.py:206
  102.2 8.0 %collective-permute-done.8.third_ref = bf16[128,512]{1,0:T(8,128)(2,1)S(1)} collective-permute-done((bf16[128,512]{1,0:T(8,128)(2,1)}, bf16[128,512]{1,0:T(8,128)(2,1)S(1)}, u32[]{:S(2)}, u32[]{:S(2)}) %collective-permute-start.8) | collective-permute-done | bytes 131104 | tf_op jit(solution)/shard_map/ppermute | solution.py:206
  110.2 12.0 %shard_map.146 = (bf16[272,512]{1,0:T(8,128)(2,1)S(1)}, bf16[128,4096]{1,0:T(8,128)(2,1)}, bf16[128,512]{1,0:T(8,128)(2,1)}) custom-call(s32[1]{0:T(128)} %bitcast.8.special, bf16[272,512]{1,0:T(8,128)(2,1)S(1)} %collective-permute-done.6.in_ref, bf16[128,512]{1,0:T(8,128)(2,1)} %collective-permute-done.7.k_ref, ...), custom_call_target="tpu_custom_call" | custom-call | flops 536870912 | bytes 4194304 | tf_op jit(solution)/shard_map/pallas_call | solution.py:192
  122.2 4.6 %collective-permute-start.10 = (bf16[272,512]{1,0:T(8,128)(2,1)S(1)}, bf16[272,512]{1,0:T(8,128)(2,1)S(1)}, u32[]{:S(2)}, u32[]{:S(2)}) collective-permute-start(bf16[272,512]{1,0:T(8,128)(2,1)S(1)} %get-tuple-element.15), channel_id=1, source_target_pairs={{0,30},{2,28},{4,26},{6,24},{8,22},{10,20},{12,18},{16,14},{18,12}... | collective-permute-start | bytes 835592 | tf_op jit(solution)/shard_map/ppermute | solution.py:292
  126.8 1.3 broadcast_select_fusion.1
  128.0 14.2 %collective-permute-done.10 = bf16[272,512]{1,0:T(8,128)(2,1)S(1)} collective-permute-done((bf16[272,512]{1,0:T(8,128)(2,1)S(1)}, bf16[272,512]{1,0:T(8,128)(2,1)S(1)}, u32[]{:S(2)}, u32[]{:S(2)}) %collective-permute-start.10) | collective-permute-done | bytes 278560 | tf_op jit(solution)/shard_map/ppermute | solution.py:292
  142.3 4.7 %shard_map.147 = bf16[128,512]{1,0:T(8,128)(2,1)S(1)} custom-call(bf16[272,512]{1,0:T(8,128)(2,1)S(1)} %broadcast_select_fusion.2.pack_ref, bf16[128,4096]{1,0:T(8,128)(2,1)S(1)} %bitcast.23, s32[128,1]{1,0:T(8,128)S(1)} %copy.17.seg_col, s32[1,128]{1,0:T(1,128)S(1)} %bitcast.33), custom_call_target="tpu_custom_call" | custom-call | flops 214748368 | bytes 4194304 | tf_op jit(solution)/shard_map/pallas_call | solution.py:192
  147.0 1.0 maximum_bitcast_fusion
  148.1 5.3 %collective-permute-done.11 = bf16[128,512]{1,0:T(8,128)(2,1)S(1)} collective-permute-done((bf16[128,512]{1,0:T(8,128)(2,1)S(1)}, bf16[128,512]{1,0:T(8,128)(2,1)S(1)}, u32[]{:S(2)}, u32[]{:S(2)}) %collective-permute-start.11) | collective-permute-done | bytes 131104 | tf_op jit(solution)/shard_map/ppermute | solution.py:206
  153.4 1.0 copy.24
  154.4 1.6 copy.25
  (33 shorter events, 2.4 us)
Async XLA Ops:
  0.6 109.6 %collective-permute-start.9 = (bf16[128,4096]{1,0:T(8,128)(2,1)}, bf16[128,4096]{1,0:T(8,128)(2,1)}, u32[]{:S(2)}, u32[]{:S(2)}) collective-permute-start(bf16[128,4096]{1,0:T(8,128)(2,1)} %bitcast.24), channel_id=1, source_target_pairs={{2,0},{4,2},{6,4},{8,6},{10,8},{12,10},{14,12},{18,16},{20,18},{22... | collective-permute-start | bytes 3145736 | tf_op jit(solution)/shard_map/ppermute | solution.py:255
  4.0 1.2 copy-start.2
  5.2 0.9 copy-start.5
  6.1 0.7 copy-start.7
  18.5 3.1 %copy-start.8 = (s32[1,128]{1,0:T(1,128)S(1)}, s32[1,128]{1,0:T(1,128)}, u32[]{:S(2)}) copy-start(s32[1,128]{1,0:T(1,128)} %seg_row.3) | copy-start | bytes 1540
  18.5 25.5 %copy-start = (bf16[1,128,4096]{2,1,0:T(8,128)(2,1)S(1)}, bf16[1,128,4096]{2,1,0:T(8,128)(2,1)}, u32[]{:S(2)}) copy-start(bf16[1,128,4096]{2,1,0:T(8,128)(2,1)} %param.13) | copy-start | bytes 3145732
  18.5 25.5 %copy-start.1 = (bf16[1,128,4096]{2,1,0:T(8,128)(2,1)S(1)}, bf16[1,128,4096]{2,1,0:T(8,128)(2,1)}, u32[]{:S(2)}) copy-start(bf16[1,128,4096]{2,1,0:T(8,128)(2,1)} %param.17) | copy-start | bytes 3145732
  19.6 107.2 %collective-permute-start = (bf16[64,4096]{1,0:T(8,128)(2,1)}, bf16[64,4096]{1,0:T(8,128)(2,1)}, u32[]{:S(2)}, u32[]{:S(2)}) collective-permute-start(bf16[64,4096]{1,0:T(8,128)(2,1)} %get-tuple-element.20), channel_id=1, source_target_pairs={{0,2},{1,3},{2,4},{3,5},{4,6},{5,7},{6,8},{7,9},{8,10},{9,11},{10,... | collective-permute-start | bytes 1572872 | tf_op jit(solution)/shard_map/ppermute | solution.py:221
  21.5 105.2 %collective-permute-start.1 = (bf16[64,4096]{1,0:T(8,128)(2,1)}, bf16[64,4096]{1,0:T(8,128)(2,1)}, u32[]{:S(2)}, u32[]{:S(2)}) collective-permute-start(bf16[64,4096]{1,0:T(8,128)(2,1)} %get-tuple-element.19), channel_id=1, source_target_pairs={{0,3},{1,2},{2,5},{3,4},{4,7},{5,6},{6,9},{7,8},{8,11},{9,10},{10,... | collective-permute-start | bytes 1572872 | tf_op jit(solution)/shard_map/ppermute | solution.py:221
  21.5 31.1 %collective-permute-start.7 = (bf16[128,512]{1,0:T(8,128)(2,1)}, bf16[128,512]{1,0:T(8,128)(2,1)}, u32[]{:S(2)}, u32[]{:S(2)}) collective-permute-start(bf16[128,512]{1,0:T(8,128)(2,1)} %bitcast.11.k_ref), channel_id=1, source_target_pairs={{0,30},{2,28},{4,26},{6,24},{8,22},{10,20},{12,18},{14,16},{16,14}... | collective-permute-start | bytes 393224 | tf_op jit(solution)/shard_map/ppermute | solution.py:206
  21.5 19.0 %collective-permute-start.5 = (s32[128]{0:T(128)S(1)}, s32[128]{0:T(128)S(1)}, u32[]{:S(2)}, u32[]{:S(2)}) collective-permute-start(s32[128]{0:T(128)S(1)} %bitcast.35), channel_id=1, source_target_pairs={{0,30},{2,28},{4,26},{6,24},{8,22},{10,20},{12,18},{14,16},{16,14}... | collective-permute-start | bytes 1544 | tf_op jit(solution)/shard_map/ppermute | solution.py:206
  40.5 12.1 %collective-permute-start.3 = (bf16[128,512]{1,0:T(8,128)(2,1)}, bf16[128,512]{1,0:T(8,128)(2,1)}, u32[]{:S(2)}, u32[]{:S(2)}) collective-permute-start(bf16[128,512]{1,0:T(8,128)(2,1)} %bitcast.1.k_ref), channel_id=1, source_target_pairs={{0,30},{2,28},{4,26},{6,24},{8,22},{10,20},{12,18},{14,16},{16,14}... | collective-permute-start | bytes 393224 | tf_op jit(solution)/shard_map/ppermute | solution.py:206
  44.0 0.9 copy-start.4
  44.9 7.7 %copy-start.6 = (bf16[1,128,512]{2,1,0:T(8,128)(2,1)S(1)}, bf16[1,128,512]{2,1,0:T(8,128)(2,1)}, u32[]{:S(2)}) copy-start(bf16[1,128,512]{2,1,0:T(8,128)(2,1)} %param.11) | copy-start | bytes 393220
  44.9 65.2 %copy-start.3 = (bf16[1,128,4096]{2,1,0:T(8,128)(2,1)S(1)}, bf16[1,128,4096]{2,1,0:T(8,128)(2,1)}, u32[]{:S(2)}) copy-start(bf16[1,128,4096]{2,1,0:T(8,128)(2,1)} %param.9) | copy-start | bytes 3145732
  52.6 57.5 %collective-permute-start.6 = (bf16[272,512]{1,0:T(8,128)(2,1)S(1)}, bf16[272,512]{1,0:T(8,128)(2,1)S(1)}, u32[]{:S(2)}, u32[]{:S(2)}) collective-permute-start(bf16[272,512]{1,0:T(8,128)(2,1)S(1)} %get-tuple-element.12), channel_id=1, source_target_pairs={{0,30},{2,28},{4,26},{6,24},{8,22},{10,20},{12,18},{14,16},{16,14}... | collective-permute-start | bytes 835592 | tf_op jit(solution)/shard_map/ppermute | solution.py:206
  52.7 49.4 %collective-permute-start.4 = (bf16[128,512]{1,0:T(8,128)(2,1)S(1)}, bf16[128,512]{1,0:T(8,128)(2,1)S(1)}, u32[]{:S(2)}, u32[]{:S(2)}) collective-permute-start(bf16[128,512]{1,0:T(8,128)(2,1)S(1)} %bitcast.30), channel_id=1, source_target_pairs={{0,30},{2,28},{4,26},{6,24},{8,22},{10,20},{12,18},{14,16},{16,14}... | collective-permute-start | bytes 393224 | tf_op jit(solution)/shard_map/ppermute | solution.py:206
  102.1 8.1 %collective-permute-start.8 = (bf16[128,512]{1,0:T(8,128)(2,1)}, bf16[128,512]{1,0:T(8,128)(2,1)S(1)}, u32[]{:S(2)}, u32[]{:S(2)}) collective-permute-start(bf16[128,512]{1,0:T(8,128)(2,1)} %get-tuple-element.13), channel_id=1, source_target_pairs={{0,30},{2,28},{4,26},{6,24},{8,22},{10,20},{12,18},{14,16},{16,14}... | collective-permute-start | bytes 393224 | tf_op jit(solution)/shard_map/ppermute | solution.py:206
  110.2 37.9 %collective-permute-start.2 = (bf16[128,4096]{1,0:T(8,128)(2,1)S(1)}, bf16[128,4096]{1,0:T(8,128)(2,1)S(1)}, u32[]{:S(2)}, u32[]{:S(2)}) collective-permute-start(bf16[128,4096]{1,0:T(8,128)(2,1)S(1)} %bitcast.27), channel_id=1, source_target_pairs={{0,30},{2,28},{4,26},{6,24},{8,22},{10,20},{12,18},{14,16},{16,14}... | collective-permute-start | bytes 3145736 | tf_op jit(solution)/shard_map/ppermute | solution.py:206
  122.2 20.0 %collective-permute-start.10 = (bf16[272,512]{1,0:T(8,128)(2,1)S(1)}, bf16[272,512]{1,0:T(8,128)(2,1)S(1)}, u32[]{:S(2)}, u32[]{:S(2)}) collective-permute-start(bf16[272,512]{1,0:T(8,128)(2,1)S(1)} %get-tuple-element.15), channel_id=1, source_target_pairs={{0,30},{2,28},{4,26},{6,24},{8,22},{10,20},{12,18},{16,14},{18,12}... | collective-permute-start | bytes 835592 | tf_op jit(solution)/shard_map/ppermute | solution.py:292
  146.9 6.5 %collective-permute-start.11 = (bf16[128,512]{1,0:T(8,128)(2,1)S(1)}, bf16[128,512]{1,0:T(8,128)(2,1)S(1)}, u32[]{:S(2)}, u32[]{:S(2)}) collective-permute-start(bf16[128,512]{1,0:T(8,128)(2,1)S(1)} %shard_map.147), channel_id=1, source_target_pairs={{0,30},{2,28},{4,26},{6,24},{8,22},{10,20},{12,18},{14,16},{16,14}... | collective-permute-start | bytes 393224 | tf_op jit(solution)/shard_map/ppermute | solution.py:206

commit v3 on v1

v3 whole, which is shorter than its diff:
```python
import functools

import jax
import jax.numpy as jnp
from jax import lax
from jax.experimental import pallas as pl
from jax.experimental.pallas import tpu as pltpu
from jax.sharding import PartitionSpec as P

HQ = 64
KV = 8
HD = 128
GROUP = HQ // KV
SCALE = HD**-0.5
LOW = jnp.bfloat16
F32 = jnp.float32
DIAG_ROWS = 16
MESH = pl.DeviceIdType.MESH


def dot_nt(a, b):
    return lax.dot_general(a, b, (((1,), (1,)), ((), ())), preferred_element_type=F32)


def dot_tn(a, b):
    return lax.dot_general(a, b, (((0,), (0,)), ((), ())), preferred_element_type=F32)


def dot_nn(a, b):
    return lax.dot_general(a, b, (((1,), (0,)), ((), ())), preferred_element_type=F32)


def iotas(shape):
    return lax.broadcasted_iota(jnp.int32, shape, 0), lax.broadcasted_iota(jnp.int32, shape, 1)


def segment_sides(ids_ref):
    tokens = ids_ref.shape[1]
    across = jnp.broadcast_to(ids_ref[...].astype(F32), (tokens, tokens))
    return across.T, across


def allowed_mask(down, across):
    rows, cols = iotas(down.shape)
    return (down == across) & (cols <= rows)


def probability(q, k, allowed):
    scores = jnp.where(allowed, dot_nt(q, k) * SCALE, -jnp.inf)
    weights = jnp.exp(scores - jnp.max(scores, axis=1, keepdims=True))
    return weights / jnp.sum(weights, axis=1, keepdims=True)


def pack(full):
    half = full.shape[0] // 2
    rows, cols = iotas((half, half))
    turned = full[half:, :].T
    packed = full[:half, :half] + turned[:half] + jnp.where(rows < cols, turned[half:], 0.0)
    diag = jnp.sum(jnp.where(rows == cols, full[half:, half:], 0.0), axis=0, keepdims=True)
    return packed, diag


def unpack_masks(down, across):
    half = down.shape[0] // 2
    rows, cols = iotas((half, half))
    first = (down[:half, :half] == across[:half, :half]) & (cols <= rows)
    cross = down[:half, :half] == across[:half, half:]
    second = (down[half:, half:] == across[half:, half:]) & (rows < cols)
    return first, jnp.concatenate([cross, second], axis=0), rows == cols


def unpack(packed, diag, masks):
    first, turned_mask, eye = masks
    turned = jnp.where(turned_mask, jnp.concatenate([packed, packed], axis=0), 0.0).T
    half = packed.shape[0]
    zero = jnp.zeros((half, half), F32)
    on_diag = jnp.where(eye, jnp.broadcast_to(diag, (half, half)), 0.0)
    top = jnp.concatenate([jnp.where(first, packed, 0.0), zero], axis=1)
    bottom = turned + jnp.concatenate([zero, on_diag], axis=1)
    return jnp.concatenate([top, bottom], axis=0)


def store_packed(g, parts, diag_scratch, pack_ref):
    half = parts[0][0].shape[0]
    values = jnp.concatenate([p for p, _ in parts], axis=1).astype(LOW)
    pack_ref[pl.ds(pl.multiple_of(g * half, half), half), :] = values
    diags = jnp.concatenate([d for _, d in parts], axis=1)
    rows, _ = iotas(diag_scratch.shape)
    diag_scratch[...] = jnp.where(rows == g, jnp.broadcast_to(diags, rows.shape), diag_scratch[...])


def load_packed(g, pack_ref):
    half = pack_ref.shape[1] // GROUP
    values = pack_ref[pl.ds(pl.multiple_of(g * half, half), half), :].astype(F32)
    tail = pack_ref[pl.ds(pack_ref.shape[0] - DIAG_ROWS, DIAG_ROWS), :].astype(F32)
    rows, _ = iotas(tail.shape)
    diags = jnp.sum(jnp.where(rows == g, tail, 0.0), axis=0, keepdims=True)
    return [
        (values[:, h * half : (h + 1) * half], diags[:, h * half : (h + 1) * half]) for h in range(GROUP)
    ]


def head(g, h):
    return pl.ds(pl.multiple_of((g * GROUP + h) * HD, HD), HD)


def own(g):
    return pl.ds(pl.multiple_of(g * HD, HD), HD)


def score_gradient(prob, grad, v):
    dprob = dot_nt(grad, v)
    delta = jnp.sum(prob * dprob, axis=1, keepdims=True)
    return prob * (dprob - delta) * SCALE


def every_group(kv_local, body):
    lax.fori_loop(0, kv_local, lambda g, carry: (body(g), carry)[1], 0)


def tick(
    sections, splits,
    fwd_q, fwd_k, fwd_v, fwd_ids, held_q, held_k, held_v, back_ids, up_grad,
    passed, evicted_q, evicted_k, evicted_v, grad_q, grad_k, grad_v,
    fq, fk, fv, fids, hq, hk, hv, bids, ug,
    out, holder_ids, keys, third, third_in, arriving, pack_out, pack_in, score_out, score_in, gk, diag,
    load_sem, send_sem, recv_sem, out_send, out_recv,
):
    me, lane = lax.axis_index("section"), lax.axis_index("tp")
    mirror = sections - 1 - me
    right, left = lax.rem(me + 1, sections), lax.rem(me + sections - 1, sections)
    section_short = right == mirror
    holder_short = lax.rem(mirror + 1, sections) == me
    tokens = hq.shape[0]
    kv_local = hk.shape[1] // HD
    rows = tokens // splits
    width = hq.shape[1]

    pairs = [(held_q, hq), (held_k, hk), (held_v, hv), (up_grad, ug), (fwd_q, fq), (fwd_k, fk), (fwd_v, fv),
             (fwd_ids, fids), (back_ids, bids)]
    loads = [pltpu.make_async_copy(src, dst, load_sem.at[n]) for n, (src, dst) in enumerate(pairs)]
    for load in loads:
        load.start()

    barrier = pltpu.get_barrier_semaphore()
    pl.semaphore_signal(barrier, inc=1, device_id=(mirror, lane), device_id_type=MESH)
    for t in range(splits):
        pl.semaphore_signal(barrier, inc=1, device_id=(left, t), device_id_type=MESH)
        pl.semaphore_signal(barrier, inc=1, device_id=(right, t), device_id_type=MESH)
    pl.semaphore_wait(barrier, 1 + 2 * splits)

    def remote(n, src, dst, section):
        return pltpu.make_async_remote_copy(
            src_ref=src, dst_ref=dst, send_sem=send_sem.at[n], recv_sem=recv_sem.at[n],
            device_id=(section, lane), device_id_type=MESH,
        )

    chunk = tokens // 4
    send_ids = remote(0, back_ids, holder_ids, mirror)
    send_keys = remote(1, held_k, keys, mirror)
    send_ek = remote(2, fwd_k, evicted_k, mirror)
    send_ev = remote(3, fwd_v, evicted_v, mirror)
    send_pack = remote(4, pack_out, pack_in, mirror)
    send_third = remote(5, third, third_in, mirror)
    send_score = remote(6, score_out, score_in, mirror)
    send_gk = remote(7, gk, grad_k, mirror)
    send_up = remote(8, up_grad, arriving, left)
    send_eq = [
        remote(9 + c, fwd_q.at[pl.ds(c * chunk, chunk)], evicted_q.at[pl.ds(c * chunk, chunk)], mirror)
        for c in range(4)
    ]
    send_out = []
    for offset in range(splits):
        to = lax.rem(lane + offset, splits)
        send_out.append(
            pltpu.make_async_remote_copy(
                src_ref=out.at[pl.ds(pl.multiple_of(to * rows, rows), rows)],
                dst_ref=passed.at[:, pl.ds(pl.multiple_of(lane * width, width), width)],
                send_sem=out_send.at[offset], recv_sem=out_recv.at[offset],
                device_id=(right, to), device_id_type=MESH,
            )
        )

    send_ids.start()
    send_keys.start()
    send_ek.start()

    @pl.when(jnp.logical_not(holder_short))
    def _():
        send_up.start()

    diag[...] = jnp.zeros(diag.shape, F32)

    def close_pack(ref):
        ref[pl.ds(ref.shape[0] - DIAG_ROWS, DIAG_ROWS), :] = diag[...].astype(LOW)

    for load in loads[:4]:
        load.wait()
    send_ids.wait_recv()

    @pl.when(jnp.logical_not(holder_short))
    def _():
        allowed = allowed_mask(*segment_sides(holder_ids))

        def group(g):
            k = hk[:, own(g)]
            parts = [pack(probability(hq[:, head(g, h)], k, allowed)) for h in range(GROUP)]
            store_packed(g, parts, diag, pack_out)

        every_group(kv_local, group)
        third[...] = hv[...]

    @pl.when(holder_short)
    def _():
        allowed = allowed_mask(*segment_sides(holder_ids))

        def group(g):
            k, v = hk[:, own(g)], hv[:, own(g)]
            total = jnp.zeros((tokens, HD), F32)
            parts = []
            for h in range(GROUP):
                prob = probability(hq[:, head(g, h)], k, allowed)
                grad = ug[:, head(g, h)]
                total = total + dot_tn(prob.astype(LOW), grad)
                parts.append(pack(score_gradient(prob, grad, v)))
            store_packed(g, parts, diag, pack_out)
            third[:, own(g)] = total.astype(LOW)

        every_group(kv_local, group)

    close_pack(pack_out)
    send_pack.start()
    send_third.start()
    send_ev.start()
    send_eq[0].start()
    send_eq[1].start()

    for load in loads[4:]:
        load.wait()
    forward_allowed = allowed_mask(*segment_sides(fids))

    def forward_group(g):
        k, v = fk[:, own(g)], fv[:, own(g)]
        for h in range(GROUP):
            prob = probability(fq[:, head(g, h)], k, forward_allowed)
            out[:, head(g, h)] = dot_nn(prob.astype(LOW), v).astype(LOW)

    every_group(kv_local, forward_group)
    for send in send_out:
        send.start()

    send_keys.wait_recv()
    send_pack.wait_recv()
    send_third.wait_recv()
    masks = unpack_masks(*segment_sides(bids))

    @pl.when(jnp.logical_not(section_short))
    def _():
        send_up.wait_recv()

        def group(g):
            k, v = keys[:, own(g)], third_in[:, own(g)]
            total = jnp.zeros((tokens, HD), F32)
            parts = []
            for h, (packed, on_diag) in enumerate(load_packed(g, pack_in)):
                prob = unpack(packed, on_diag, masks)
                grad = arriving[:, head(g, h)]
                total = total + dot_tn(prob.astype(LOW), grad)
                dscore = score_gradient(prob, grad, v)
                grad_q[:, head(g, h)] = dot_nn(dscore.astype(LOW), k).astype(LOW)
                parts.append(pack(dscore))
            store_packed(g, parts, diag, score_out)
            grad_v[:, own(g)] = total.astype(LOW)

        every_group(kv_local, group)
        close_pack(score_out)
        send_score.start()

    send_eq[2].start()

    @pl.when(section_short)
    def _():
        def group(g):
            k = keys[:, own(g)]
            for h, (packed, on_diag) in enumerate(load_packed(g, pack_in)):
                dscore = unpack(packed, on_diag, masks)
                grad_q[:, head(g, h)] = dot_nn(dscore.astype(LOW), k).astype(LOW)

        every_group(kv_local, group)
        grad_v[...] = third_in[...]

    def key_gradient(ref):
        holder_masks = unpack_masks(*segment_sides(holder_ids))

        def group(g):
            total = jnp.zeros((tokens, HD), F32)
            for h, (packed, on_diag) in enumerate(load_packed(g, ref)):
                dscore = unpack(packed, on_diag, holder_masks).astype(LOW)
                total = total + dot_tn(dscore, hq[:, head(g, h)])
            gk[:, own(g)] = total.astype(LOW)

        every_group(kv_local, group)

    @pl.when(holder_short)
    def _():
        key_gradient(pack_out)

    @pl.when(jnp.logical_not(holder_short))
    def _():
        send_score.wait_recv()
        key_gradient(score_in)

    send_gk.start()
    send_eq[3].start()

    for send in [send_ids, send_keys, send_ek, send_ev, send_pack, send_third, send_gk] + send_eq + send_out:
        send.wait_send()

    @pl.when(jnp.logical_not(holder_short))
    def _():
        send_up.wait_send()

    @pl.when(jnp.logical_not(section_short))
    def _():
        send_score.wait_send()

    for send in [send_ek, send_ev, send_gk] + send_eq + send_out:
        send.wait_recv()


def shards(fwd_q, fwd_k, fwd_v, fwd_segments, held_q, held_k, held_v, back_segments, up_grad):
    sections, splits = lax.axis_size("section"), lax.axis_size("tp")
    tokens, width = held_q.shape[1], held_q.shape[2]
    narrow_width = held_k.shape[2]
    kv_local = narrow_width // HD
    wide, narrow, ids = (tokens, width), (tokens, narrow_width), (1, tokens)
    packed = (kv_local * (tokens // 2) + DIAG_ROWS, GROUP * (tokens // 2))
    passed = (tokens // splits, splits * width)
    anywhere, vmem = pl.BlockSpec(memory_space=pl.ANY), pl.BlockSpec(memory_space=pltpu.VMEM)

    def low(*shapes):
        return [pltpu.VMEM(shape, LOW) for shape in shapes]

    def number(*shapes):
        return [pltpu.VMEM(shape, jnp.int32) for shape in shapes]

    results = pl.pallas_call(
        functools.partial(tick, sections, splits),
        in_specs=[anywhere] * 9,
        out_specs=[anywhere] * 4 + [vmem, anywhere, vmem],
        out_shape=[jax.ShapeDtypeStruct(s, LOW) for s in (passed, wide, narrow, narrow, wide, narrow, narrow)],
        scratch_shapes=low(wide, narrow, narrow) + number(ids)
        + low(wide, narrow, narrow) + number(ids) + low(wide, wide)
        + number(ids) + low(narrow, narrow, narrow, wide, packed, packed, packed, packed, narrow)
        + [pltpu.VMEM((DIAG_ROWS, packed[1]), F32)]
        + [pltpu.SemaphoreType.DMA((n,)) for n in (9, 13, 13, splits, splits)],
        compiler_params=pltpu.CompilerParams(
            collective_id=0, has_side_effects=True, vmem_limit_bytes=40 * 2**20
        ),
        cost_estimate=pl.CostEstimate(flops=2**30, bytes_accessed=2**23, transcendentals=2**20),
    )(
        fwd_q[0], fwd_k[0], fwd_v[0], fwd_segments, held_q[0], held_k[0], held_v[0], back_segments, up_grad[0]
    )
    return tuple(result[None] for result in results)


def solution(mesh):
    heads = P("section", None, "tp")
    tokens = P("section", None)
    return jax.shard_map(
        shards,
        mesh=mesh,
        in_specs=(heads, heads, heads, tokens, heads, heads, heads, tokens, heads),
        out_specs=(P("section", "tp", None),) + (heads,) * 6,
        check_vma=False,
    )
```

time: 157 us -> 126 us (0.80)
  Pallas kernels: 0 us -> 110 us
  waiting for transfers between devices: 93.9 us -> 0 us
  local copies, waits for them, and re-layouts: 33.7 us -> 13.5 us
  matrix products: 18.2 us -> 0 us
  starting transfers between devices: 8.27 us -> 0 us
    pallas_call x0 -> x1, Pallas kernels: none -> 110 us  [shards(): pl.pallas_call(functools.partial(tick, sections, splits), in_specs=[anywh...]
    ppermute x9 -> x0, waiting for transfers between devices: 93.9 us -> none  [the longest x6 93.9 us: mirrored(): lax.ppermute(value, 'section', [(j, count - 1 - j) for j in range(count)])]
    dynamic_update_slice x2 -> x0, local copies, waits for them, and re-layouts: 13.3 us -> none  [passed_on(): lax.dynamic_update_slice_in_dim(passed, piece[:, None], came_from, 1)]
    dot_general x5 -> x0, matrix products: 12.5 us -> none  [the longest x1 3.3 us: backward(): jnp.einsum('kgqs,qkgd->skd', dscore, query_heads, preferred_element_type=...]
    ppermute x9 -> x0, starting transfers between devices: 8.27 us -> none  [the longest x6 5.64 us: mirrored(): lax.ppermute(value, 'section', [(j, count - 1 - j) for j in range(count)])]
    sub x2 -> x0, matrix products: 5.73 us -> none  [probability(): weights = jnp.exp(scores - row_max)]
    broadcast_in_dim x3 -> x0, local copies, waits for them, and re-layouts: 3.31 us -> none  [the longest x2 2.31 us: passed_on(): piece[:, None]]
    another operation x3 -> x0, local copies, waits for them, and re-layouts: 1.77 us -> none  [the longest x1 1.62 us: shards(): passed_output[None]]
  transfers between devices with their start and end apart: 9 -> 0, of which waited for: 2 -> 0; matrix products, arithmetic and copies ran while one was open for 28% -> 0% of each run, Pallas kernels for 0% -> 0%
where the time goes in v3:
time: 126 us; the launch traced here: 125 us
  Pallas kernels  110 us (87%)
  local copies, waits for them, and re-layouts  13.5 us (11%)
    pallas_call x1, Pallas kernels, shards(): pl.pallas_call(functools.partial(tick, sections, splits), in_specs=[anywh...  110 us
    unnamed x25, local copies, waits for them, and re-layouts  13.5 us

profile of v3, /device:TPU:16, one launch (start us, length us, event | category | flops | bytes accessed | tf_op | source)
XLA Modules:
  0.0 124.5 jit_solution(12699797316739874530)
XLA Ops:
  0.6 0.0 copy-start.7
  0.6 0.0 copy-start.8
  0.7 0.6 copy-done.7
  1.3 0.0 copy-done.8
  1.3 0.0 copy-start
  1.3 1.2 copy-done
  2.5 0.0 copy-start.1
  2.5 1.2 copy-done.1
  3.8 0.0 copy-start.2
  3.8 1.2 copy-done.2
  5.0 0.0 copy-start.3
  5.0 0.9 copy-done.3
  5.9 0.0 copy-start.4
  5.9 0.9 copy-done.4
  6.8 0.9 copy-done.5
  7.7 0.9 copy-done.6
  8.6 110.4 %shard_map.144 = (bf16[64,8192]{1,0:T(8,128)(2,1)S(1)}, bf16[128,4096]{1,0:T(8,128)(2,1)S(1)}, bf16[128,512]{1,0:T(8,128)(2,1)S(1)}, bf16[128,512]{1,0:T(8,128)(...) custom-call(bf16[128,4096]{1,0:T(8,128)(2,1)S(1)} %bitcast.21, ...), custom_call_target="tpu_custom_call" | custom-call | flops 1073741824 | bytes 8388608 | tf_op jit(solution)/shard_map/pallas_call | solution.py:347
  119.0 1.0 copy.23
  120.0 1.0 copy.24
  120.9 0.7 copy.25
  121.6 0.7 copy.26
  122.3 1.0 copy.27
  123.2 0.7 copy.28
  123.9 0.7 copy.29
  (2 shorter events, 0.0 us)
Async XLA Ops:
  0.6 0.7 copy-start.7
  0.6 0.7 copy-start.8
  1.3 1.2 copy-start
  2.5 1.2 copy-start.1
  3.8 1.2 copy-start.2
  5.0 0.9 copy-start.3
  5.9 0.9 copy-start.4
  6.8 0.9 copy-start.5
  7.7 0.9 copy-start.6

commit v4 on v3

--- a/solution.py
+++ b/solution.py
@@ -123,8 +123,8 @@
     fwd_q, fwd_k, fwd_v, fwd_ids, held_q, held_k, held_v, back_ids, up_grad,
     passed, evicted_q, evicted_k, evicted_v, grad_q, grad_k, grad_v,
     fq, fk, fv, fids, hq, hk, hv, bids, ug,
-    out, holder_ids, keys, third, third_in, arriving, pack_out, pack_in, score_out, score_in, gk, diag,
-    load_sem, send_sem, recv_sem, out_send, out_recv,
+    out, near, holder_ids, far_ids, keys, third, third_in, arriving, pack_out, pack_in, score_out, score_in, gk, diag,
+    load_sem, send_sem, recv_sem, out_send, out_recv, near_send, near_recv,
 ):
     me, lane = lax.axis_index("section"), lax.axis_index("tp")
     mirror = sections - 1 - me
@@ -147,7 +147,10 @@
     for t in range(splits):
         pl.semaphore_signal(barrier, inc=1, device_id=(left, t), device_id_type=MESH)
         pl.semaphore_signal(barrier, inc=1, device_id=(right, t), device_id_type=MESH)
-    pl.semaphore_wait(barrier, 1 + 2 * splits)
+    for t in range(1, splits):
+        peer = lax.rem(lane + t, splits)
+        pl.semaphore_signal(barrier, inc=1, device_id=(me, peer), device_id_type=MESH)
+    pl.semaphore_wait(barrier, 3 * splits)
 
     def remote(n, src, dst, section):
         return pltpu.make_async_remote_copy(
@@ -169,7 +172,8 @@
         remote(9 + c, fwd_q.at[pl.ds(c * chunk, chunk)], evicted_q.at[pl.ds(c * chunk, chunk)], mirror)
         for c in range(4)
     ]
-    send_out = []
+    send_far = remote(13, fwd_ids, far_ids, mirror)
+    send_out, send_near = [], []
     for offset in range(splits):
         to = lax.rem(lane + offset, splits)
         send_out.append(
@@ -180,8 +184,21 @@
                 device_id=(right, to), device_id_type=MESH,
             )
         )
+        near_rows = near.at[pl.ds(pl.multiple_of(to * rows, rows), rows)]
+        columns = passed.at[:, pl.ds(pl.multiple_of(lane * width, width), width)]
+        if offset == 0:
+            send_near.append(pltpu.make_async_copy(near_rows, columns, near_send.at[0]))
+        else:
+            send_near.append(
+                pltpu.make_async_remote_copy(
+                    src_ref=near_rows, dst_ref=columns,
+                    send_sem=near_send.at[offset], recv_sem=near_recv.at[offset],
+                    device_id=(me, to), device_id_type=MESH,
+                )
+            )
 
     send_ids.start()
+    send_far.start()
     send_keys.start()
     send_ek.start()
 
@@ -235,19 +252,30 @@
     send_eq[0].start()
     send_eq[1].start()
 
+    @pl.when(section_short)
+    def _():
+        send_eq[2].start()
+        send_eq[3].start()
+
     for load in loads[4:]:
         load.wait()
-    forward_allowed = allowed_mask(*segment_sides(fids))
-
-    def forward_group(g):
-        k, v = fk[:, own(g)], fv[:, own(g)]
-        for h in range(GROUP):
-            prob = probability(fq[:, head(g, h)], k, forward_allowed)
-            out[:, head(g, h)] = dot_nn(prob.astype(LOW), v).astype(LOW)
-
-    every_group(kv_local, forward_group)
-    for send in send_out:
-        send.start()
+
+    def run_forward(ids_ref, out_ref):
+        allowed = allowed_mask(*segment_sides(ids_ref))
+
+        def group(g):
+            k, v = fk[:, own(g)], fv[:, own(g)]
+            for h in range(GROUP):
+                prob = probability(fq[:, head(g, h)], k, allowed)
+                out_ref[:, head(g, h)] = dot_nn(prob.astype(LOW), v).astype(LOW)
+
+        every_group(kv_local, group)
+
+    @pl.when(jnp.logical_not(section_short))
+    def _():
+        run_forward(fids, out)
+        for send in send_out:
+            send.start()
 
     send_keys.wait_recv()
     send_pack.wait_recv()
@@ -275,8 +303,7 @@
         every_group(kv_local, group)
         close_pack(score_out)
         send_score.start()
-
-    send_eq[2].start()
+        send_eq[2].start()
 
     @pl.when(section_short)
     def _():
@@ -311,9 +338,36 @@
         key_gradient(score_in)
 
     send_gk.start()
-    send_eq[3].start()
-
-    for send in [send_ids, send_keys, send_ek, send_ev, send_pack, send_third, send_gk] + send_eq + send_out:
+
+    @pl.when(jnp.logical_not(section_short))
+    def _():
+        send_eq[3].start()
+
+    for send in [send_ek, send_ev, send_far] + send_eq:
+        send.wait_recv()
+
+    @pl.when(holder_short)
+    def _():
+        again = [
+            pltpu.make_async_copy(src, dst, load_sem.at[4 + n])
+            for n, (src, dst) in enumerate([(evicted_q, fq), (evicted_k, fk), (evicted_v, fv)])
+        ]
+        for load in again:
+            load.start()
+        for load in again:
+            load.wait()
+        run_forward(far_ids, near)
+        for send in send_near:
+            send.start()
+        for send in send_near:
+            send.wait()
+
+    @pl.when(jnp.logical_not(holder_short))
+    def _():
+        for send in send_out:
+            send.wait_recv()
+
+    for send in [send_ids, send_far, send_keys, send_ek, send_ev, send_pack, send_third, send_gk] + send_eq:
         send.wait_send()
 
     @pl.when(jnp.logical_not(holder_short))
@@ -323,9 +377,20 @@
     @pl.when(jnp.logical_not(section_short))
     def _():
         send_score.wait_send()
-
-    for send in [send_ek, send_ev, send_gk] + send_eq + send_out:
-        send.wait_recv()
+        for send in send_out:
+            send.wait_send()
+
+    send_gk.wait_recv()
+
+
+def write_all(*refs):
+    count = len(refs) // 2
+    sems = refs[-1]
+    copies = [pltpu.make_async_copy(refs[n], refs[count + n], sems.at[n]) for n in range(count)]
+    for copy in copies:
+        copy.start()
+    for copy in copies:
+        copy.wait()
 
 
 def shards(fwd_q, fwd_k, fwd_v, fwd_segments, held_q, held_k, held_v, back_segments, up_grad):
@@ -346,21 +411,29 @@
 
     results = pl.pallas_call(
         functools.partial(tick, sections, splits),
-        in_specs=[anywhere] * 9,
+        in_specs=[pl.BlockSpec(memory_space=pltpu.HBM)] * 9,
         out_specs=[anywhere] * 4 + [vmem, anywhere, vmem],
         out_shape=[jax.ShapeDtypeStruct(s, LOW) for s in (passed, wide, narrow, narrow, wide, narrow, narrow)],
         scratch_shapes=low(wide, narrow, narrow) + number(ids)
-        + low(wide, narrow, narrow) + number(ids) + low(wide, wide)
-        + number(ids) + low(narrow, narrow, narrow, wide, packed, packed, packed, packed, narrow)
+        + low(wide, narrow, narrow) + number(ids) + low(wide, wide, wide)
+        + number(ids, ids) + low(narrow, narrow, narrow, wide, packed, packed, packed, packed, narrow)
         + [pltpu.VMEM((DIAG_ROWS, packed[1]), F32)]
-        + [pltpu.SemaphoreType.DMA((n,)) for n in (9, 13, 13, splits, splits)],
+        + [pltpu.SemaphoreType.DMA((n,)) for n in (9, 14, 14) + (splits,) * 4],
         compiler_params=pltpu.CompilerParams(
-            collective_id=0, has_side_effects=True, vmem_limit_bytes=40 * 2**20
+            collective_id=0, has_side_effects=True, vmem_limit_bytes=60 * 2**20
         ),
         cost_estimate=pl.CostEstimate(flops=2**30, bytes_accessed=2**23, transcendentals=2**20),
     )(
         fwd_q[0], fwd_k[0], fwd_v[0], fwd_segments, held_q[0], held_k[0], held_v[0], back_segments, up_grad[0]
     )
+    results = pl.pallas_call(
+        write_all,
+        in_specs=[anywhere] * 7,
+        out_specs=[pl.BlockSpec(memory_space=pltpu.HBM)] * 7,
+        out_shape=[jax.ShapeDtypeStruct(result.shape, LOW) for result in results],
+        scratch_shapes=[pltpu.SemaphoreType.DMA((7,))],
+        compiler_params=pltpu.CompilerParams(vmem_limit_bytes=60 * 2**20),
+    )(*results)
     return tuple(result[None] for result in results)
 
 

time: 126 us -> 224 us (1.78)
  Pallas kernels: 110 us -> 223 us
  local copies, waits for them, and re-layouts: 13.5 us -> 0 us
    pallas_call x1 -> x2, Pallas kernels: 110 us -> 223 us  [the longest x1 112 us: shards(): pl.pallas_call(write_all, in_specs=[anywhere] * 7, out_specs=[pl.BlockSpe...]
    unnamed x25 -> x0, local copies, waits for them, and re-layouts: 13.5 us -> none
where the time goes in v4:
time: 224 us
  Pallas kernels  223 us (100%)
    pallas_call x1, Pallas kernels, shards(): pl.pallas_call(write_all, in_specs=[anywhere] * 7, out_specs=[pl.BlockSpe...  112 us
    pallas_call x1, Pallas kernels, shards(): pl.pallas_call(functools.partial(tick, sections, splits), in_specs=[pl.Bl...  111 us

profile of v4, /device:TPU:16, one launch (start us, length us, event | category | flops | bytes accessed | tf_op | source)
XLA Modules:
  0.0 223.6 jit_solution(16983670877399140621)
XLA Ops:
  0.6 110.6 %shard_map.144 = (bf16[64,8192]{1,0:T(8,128)(2,1)}, bf16[128,4096]{1,0:T(8,128)(2,1)}, bf16[128,512]{1,0:T(8,128)(2,1)}, bf16[128,512]{1,0:T(8,128)(2,1)}, bf16[...) custom-call(bf16[128,4096]{1,0:T(8,128)(2,1)} %bitcast.14, bf16[128,512]{1,0:T(8,128)(2,1)} %bitcast.20, ...), custom_call_target="tpu_custom_call" | custom-call | flops 1073741824 | bytes 8388608 | tf_op jit(solution)/shard_map/pallas_call | solution.py:412
  111.2 112.3 %shard_map.145 = (bf16[64,8192]{1,0:T(8,128)(2,1)}, bf16[128,4096]{1,0:T(8,128)(2,1)}, bf16[128,512]{1,0:T(8,128)(2,1)}, bf16[128,512]{1,0:T(8,128)(2,1)}, bf16[...) custom-call(bf16[64,8192]{1,0:T(8,128)(2,1)} %get-tuple-element.21.refs_0_, ...), custom_call_target="tpu_custom_call" | custom-call | tf_op jit(solution)/shard_map/pallas_call | solution.py:429

commit v5 on v4

--- a/solution.py
+++ b/solution.py
@@ -14,7 +14,6 @@
 SCALE = HD**-0.5
 LOW = jnp.bfloat16
 F32 = jnp.float32
-DIAG_ROWS = 16
 MESH = pl.DeviceIdType.MESH
 
 
@@ -80,21 +79,33 @@
     return jnp.concatenate([top, bottom], axis=0)
 
 
+def diag_rows(kv_local, tokens):
+    rows = kv_local * GROUP * (tokens // 2) // HD
+    return -(-rows // 16) * 16
+
+
 def store_packed(g, parts, diag_scratch, pack_ref):
     half = parts[0][0].shape[0]
     values = jnp.concatenate([p for p, _ in parts], axis=1).astype(LOW)
     pack_ref[pl.ds(pl.multiple_of(g * half, half), half), :] = values
     diags = jnp.concatenate([d for _, d in parts], axis=1)
     rows, _ = iotas(diag_scratch.shape)
-    diag_scratch[...] = jnp.where(rows == g, jnp.broadcast_to(diags, rows.shape), diag_scratch[...])
-
-
-def load_packed(g, pack_ref):
+    merged = diag_scratch[...]
+    lines = diags.shape[1] // HD
+    for c in range(lines):
+        line = jnp.broadcast_to(diags[:, c * HD : (c + 1) * HD], rows.shape)
+        merged = jnp.where(rows == g * lines + c, line, merged)
+    diag_scratch[...] = merged
+
+
+def load_packed(g, pack_ref, diag_ref):
     half = pack_ref.shape[1] // GROUP
     values = pack_ref[pl.ds(pl.multiple_of(g * half, half), half), :].astype(F32)
-    tail = pack_ref[pl.ds(pack_ref.shape[0] - DIAG_ROWS, DIAG_ROWS), :].astype(F32)
+    tail = diag_ref[...].astype(F32)
     rows, _ = iotas(tail.shape)
-    diags = jnp.sum(jnp.where(rows == g, tail, 0.0), axis=0, keepdims=True)
+    lines = pack_ref.shape[1] // HD
+    found = [jnp.sum(jnp.where(rows == g * lines + c, tail, 0.0), axis=0, keepdims=True) for c in range(lines)]
+    diags = jnp.concatenate(found, axis=1)
     return [
         (values[:, h * half : (h + 1) * half], diags[:, h * half : (h + 1) * half]) for h in range(GROUP)
     ]
@@ -123,7 +134,7 @@
     fwd_q, fwd_k, fwd_v, fwd_ids, held_q, held_k, held_v, back_ids, up_grad,
     passed, evicted_q, evicted_k, evicted_v, grad_q, grad_k, grad_v,
     fq, fk, fv, fids, hq, hk, hv, bids, ug,
-    out, near, holder_ids, far_ids, keys, third, third_in, arriving, pack_out, pack_in, score_out, score_in, gk, diag,
+    out, near, holder_ids, far_ids, keys, third, third_in, arriving, pack_out, pack_in, score_out, score_in, pack_dout, pack_din, score_dout, score_din, gk, diag,
     load_sem, send_sem, recv_sem, out_send, out_recv, near_send, near_recv,
 ):
     me, lane = lax.axis_index("section"), lax.axis_index("tp")
@@ -158,7 +169,10 @@
             device_id=(section, lane), device_id_type=MESH,
         )
 
-    chunk = tokens // 4
+
+    def block(g, base=0):
+        return pl.ds(pl.multiple_of(base + g * GROUP * HD, GROUP * HD), GROUP * HD)
+
     send_ids = remote(0, back_ids, holder_ids, mirror)
     send_keys = remote(1, held_k, keys, mirror)
     send_ek = remote(2, fwd_k, evicted_k, mirror)
@@ -168,12 +182,12 @@
     send_score = remote(6, score_out, score_in, mirror)
     send_gk = remote(7, gk, grad_k, mirror)
     send_up = remote(8, up_grad, arriving, left)
-    send_eq = [
-        remote(9 + c, fwd_q.at[pl.ds(c * chunk, chunk)], evicted_q.at[pl.ds(c * chunk, chunk)], mirror)
-        for c in range(4)
-    ]
-    send_far = remote(13, fwd_ids, far_ids, mirror)
-    send_out, send_near = [], []
+    send_pack_diag = remote(9, pack_dout, pack_din, mirror)
+    send_score_diag = remote(10, score_dout, score_din, mirror)
+    send_eq = [remote(12 + g, fwd_q.at[:, block(g)], evicted_q.at[:, block(g)], mirror) for g in range(kv_local)]
+    early, middle = (kv_local + 1) // 2, (3 * kv_local + 3) // 4
+    send_far = remote(11, fwd_ids, far_ids, mirror)
+    send_out = []
     for offset in range(splits):
         to = lax.rem(lane + offset, splits)
         send_out.append(
@@ -184,32 +198,36 @@
                 device_id=(right, to), device_id_type=MESH,
             )
         )
-        near_rows = near.at[pl.ds(pl.multiple_of(to * rows, rows), rows)]
-        columns = passed.at[:, pl.ds(pl.multiple_of(lane * width, width), width)]
-        if offset == 0:
-            send_near.append(pltpu.make_async_copy(near_rows, columns, near_send.at[0]))
-        else:
-            send_near.append(
-                pltpu.make_async_remote_copy(
-                    src_ref=near_rows, dst_ref=columns,
-                    send_sem=near_send.at[offset], recv_sem=near_recv.at[offset],
-                    device_id=(me, to), device_id_type=MESH,
+
+    def near_copies(g):
+        copies = []
+        for offset in range(splits):
+            to = lax.rem(lane + offset, splits)
+            src = near.at[pl.ds(pl.multiple_of(to * rows, rows), rows), block(g)]
+            dst = passed.at[:, block(g, lane * width)]
+            n = offset * kv_local + g
+            if offset == 0:
+                copies.append(pltpu.make_async_copy(src, dst, near_send.at[n]))
+            else:
+                copies.append(
+                    pltpu.make_async_remote_copy(
+                        src_ref=src, dst_ref=dst, send_sem=near_send.at[n], recv_sem=near_recv.at[n],
+                        device_id=(me, to), device_id_type=MESH,
+                    )
                 )
-            )
+        return copies
 
     send_ids.start()
     send_far.start()
     send_keys.start()
     send_ek.start()
+    send_ev.start()
 
     @pl.when(jnp.logical_not(holder_short))
     def _():
         send_up.start()
 
     diag[...] = jnp.zeros(diag.shape, F32)
-
-    def close_pack(ref):
-        ref[pl.ds(ref.shape[0] - DIAG_ROWS, DIAG_ROWS), :] = diag[...].astype(LOW)
 
     for load in loads[:4]:
         load.wait()
@@ -245,40 +263,36 @@
 
         every_group(kv_local, group)
 
-    close_pack(pack_out)
+    pack_dout[...] = diag[...].astype(LOW)
     send_pack.start()
+    send_pack_diag.start()
     send_third.start()
-    send_ev.start()
-    send_eq[0].start()
-    send_eq[1].start()
+    for send in send_eq[:early]:
+        send.start()
 
     @pl.when(section_short)
     def _():
-        send_eq[2].start()
-        send_eq[3].start()
+        for send in send_eq[early:]:
+            send.start()
 
     for load in loads[4:]:
         load.wait()
 
-    def run_forward(ids_ref, out_ref):
-        allowed = allowed_mask(*segment_sides(ids_ref))
-
-        def group(g):
-            k, v = fk[:, own(g)], fv[:, own(g)]
-            for h in range(GROUP):
-                prob = probability(fq[:, head(g, h)], k, allowed)
-                out_ref[:, head(g, h)] = dot_nn(prob.astype(LOW), v).astype(LOW)
-
-        every_group(kv_local, group)
+    def forward_group(allowed, out_ref, g):
+        k, v = fk[:, own(g)], fv[:, own(g)]
+        for h in range(GROUP):
+            prob = probability(fq[:, head(g, h)], k, allowed)
+            out_ref[:, head(g, h)] = dot_nn(prob.astype(LOW), v).astype(LOW)
 
     @pl.when(jnp.logical_not(section_short))
     def _():
-        run_forward(fids, out)
+        every_group(kv_local, functools.partial(forward_group, allowed_mask(*segment_sides(fids)), out))
         for send in send_out:
             send.start()
 
     send_keys.wait_recv()
     send_pack.wait_recv()
+    send_pack_diag.wait_recv()
     send_third.wait_recv()
     masks = unpack_masks(*segment_sides(bids))
 
@@ -290,7 +304,7 @@
             k, v = keys[:, own(g)], third_in[:, own(g)]
             total = jnp.zeros((tokens, HD), F32)
             parts = []
-            for h, (packed, on_diag) in enumerate(load_packed(g, pack_in)):
+            for h, (packed, on_diag) in enumerate(load_packed(g, pack_in, pack_din)):
                 prob = unpack(packed, on_diag, masks)
                 grad = arriving[:, head(g, h)]
                 total = total + dot_tn(prob.astype(LOW), grad)
@@ -301,27 +315,29 @@
             grad_v[:, own(g)] = total.astype(LOW)
 
         every_group(kv_local, group)
-        close_pack(score_out)
+        score_dout[...] = diag[...].astype(LOW)
         send_score.start()
-        send_eq[2].start()
+        send_score_diag.start()
+        for send in send_eq[early:middle]:
+            send.start()
 
     @pl.when(section_short)
     def _():
         def group(g):
             k = keys[:, own(g)]
-            for h, (packed, on_diag) in enumerate(load_packed(g, pack_in)):
+            for h, (packed, on_diag) in enumerate(load_packed(g, pack_in, pack_din)):
                 dscore = unpack(packed, on_diag, masks)
                 grad_q[:, head(g, h)] = dot_nn(dscore.astype(LOW), k).astype(LOW)
 
         every_group(kv_local, group)
         grad_v[...] = third_in[...]
 
-    def key_gradient(ref):
+    def key_gradient(ref, diag_ref):
         holder_masks = unpack_masks(*segment_sides(holder_ids))
 
         def group(g):
             total = jnp.zeros((tokens, HD), F32)
-            for h, (packed, on_diag) in enumerate(load_packed(g, ref)):
+            for h, (packed, on_diag) in enumerate(load_packed(g, ref, diag_ref)):
                 dscore = unpack(packed, on_diag, holder_masks).astype(LOW)
                 total = total + dot_tn(dscore, hq[:, head(g, h)])
             gk[:, own(g)] = total.astype(LOW)
@@ -330,44 +346,58 @@
 
     @pl.when(holder_short)
     def _():
-        key_gradient(pack_out)
+        key_gradient(pack_out, pack_dout)
 
     @pl.when(jnp.logical_not(holder_short))
     def _():
         send_score.wait_recv()
-        key_gradient(score_in)
+        send_score_diag.wait_recv()
+        key_gradient(score_in, score_din)
 
     send_gk.start()
 
     @pl.when(jnp.logical_not(section_short))
     def _():
-        send_eq[3].start()
-
-    for send in [send_ek, send_ev, send_far] + send_eq:
+        for send in send_eq[middle:]:
+            send.start()
+
+    for send in [send_ek, send_ev, send_far]:
         send.wait_recv()
 
     @pl.when(holder_short)
     def _():
         again = [
             pltpu.make_async_copy(src, dst, load_sem.at[4 + n])
-            for n, (src, dst) in enumerate([(evicted_q, fq), (evicted_k, fk), (evicted_v, fv)])
+            for n, (src, dst) in enumerate([(evicted_k, fk), (evicted_v, fv)])
         ]
         for load in again:
             load.start()
         for load in again:
             load.wait()
-        run_forward(far_ids, near)
-        for send in send_near:
-            send.start()
-        for send in send_near:
-            send.wait()
+        allowed = allowed_mask(*segment_sides(far_ids))
+        for g in range(kv_local):
+            send_eq[g].wait_recv()
+            load = pltpu.make_async_copy(evicted_q.at[:, block(g)], fq.at[:, block(g)], load_sem.at[6])
+            load.start()
+            load.wait()
+            forward_group(allowed, near, g)
+            for copy in near_copies(g):
+                copy.start()
+        for g in range(kv_local):
+            for copy in near_copies(g):
+                copy.wait()
+
+    @pl.when(jnp.logical_not(holder_short))
+    def _():
+        for send in send_eq:
+            send.wait_recv()
 
     @pl.when(jnp.logical_not(holder_short))
     def _():
         for send in send_out:
             send.wait_recv()
 
-    for send in [send_ids, send_far, send_keys, send_ek, send_ev, send_pack, send_third, send_gk] + send_eq:
+    for send in [send_ids, send_far, send_keys, send_ek, send_ev, send_pack, send_pack_diag, send_third, send_gk] + send_eq:
         send.wait_send()
 
     @pl.when(jnp.logical_not(holder_short))
@@ -377,6 +407,7 @@
     @pl.when(jnp.logical_not(section_short))
     def _():
         send_score.wait_send()
+        send_score_diag.wait_send()
         for send in send_out:
             send.wait_send()
 
@@ -384,13 +415,18 @@
 
 
 def write_all(*refs):
-    count = len(refs) // 2
-    sems = refs[-1]
-    copies = [pltpu.make_async_copy(refs[n], refs[count + n], sems.at[n]) for n in range(count)]
-    for copy in copies:
-        copy.start()
-    for copy in copies:
-        copy.wait()
+    count = (len(refs) - 2) // 3
+    here, there, rooms = refs[:count], refs[count : 2 * count], refs[2 * count : 3 * count]
+    in_sem, out_sem = refs[3 * count :]
+    reads = [pltpu.make_async_copy(here[n], rooms[n], in_sem.at[n]) for n in range(count)]
+    writes = [pltpu.make_async_copy(rooms[n], there[n], out_sem.at[n]) for n in range(count)]
+    for read in reads:
+        read.start()
+    for read, write in zip(reads, writes):
+        read.wait()
+        write.start()
+    for write in writes:
+        write.wait()
 
 
 def shards(fwd_q, fwd_k, fwd_v, fwd_segments, held_q, held_k, held_v, back_segments, up_grad):
@@ -399,7 +435,8 @@
     narrow_width = held_k.shape[2]
     kv_local = narrow_width // HD
     wide, narrow, ids = (tokens, width), (tokens, narrow_width), (1, tokens)
-    packed = (kv_local * (tokens // 2) + DIAG_ROWS, GROUP * (tokens // 2))
+    packed = (kv_local * (tokens // 2), GROUP * (tokens // 2))
+    diags = (diag_rows(kv_local, tokens), HD)
     passed = (tokens // splits, splits * width)
     anywhere, vmem = pl.BlockSpec(memory_space=pl.ANY), pl.BlockSpec(memory_space=pltpu.VMEM)
 
@@ -416,9 +453,9 @@
         out_shape=[jax.ShapeDtypeStruct(s, LOW) for s in (passed, wide, narrow, narrow, wide, narrow, narrow)],
         scratch_shapes=low(wide, narrow, narrow) + number(ids)
         + low(wide, narrow, narrow) + number(ids) + low(wide, wide, wide)
-        + number(ids, ids) + low(narrow, narrow, narrow, wide, packed, packed, packed, packed, narrow)
-        + [pltpu.VMEM((DIAG_ROWS, packed[1]), F32)]
-        + [pltpu.SemaphoreType.DMA((n,)) for n in (9, 14, 14) + (splits,) * 4],
+        + number(ids, ids) + low(narrow, narrow, narrow, wide, packed, packed, packed, packed, diags, diags, diags, diags, narrow)
+        + [pltpu.VMEM(diags, F32)]
+        + [pltpu.SemaphoreType.DMA((n,)) for n in (9, 12 + kv_local, 12 + kv_local, splits, splits, splits * kv_local, splits * kv_local)],
         compiler_params=pltpu.CompilerParams(
             collective_id=0, has_side_effects=True, vmem_limit_bytes=60 * 2**20
         ),
@@ -431,7 +468,7 @@
         in_specs=[anywhere] * 7,
         out_specs=[pl.BlockSpec(memory_space=pltpu.HBM)] * 7,
         out_shape=[jax.ShapeDtypeStruct(result.shape, LOW) for result in results],
-        scratch_shapes=[pltpu.SemaphoreType.DMA((7,))],
+        scratch_shapes=[pltpu.VMEM(result.shape, LOW) for result in results] + [pltpu.SemaphoreType.DMA((7,))] * 2,
         compiler_params=pltpu.CompilerParams(vmem_limit_bytes=60 * 2**20),
     )(*results)
     return tuple(result[None] for result in results)

time: 224 us -> 111 us (0.50)
  the two profiles are of different devices: /device:TPU:16 before, /device:TPU:11 now
where the time goes in v5:
time: 111 us; the launch traced here: 110 us
  Pallas kernels  110 us (99%)
    pallas_call x1, Pallas kernels, shards(): pl.pallas_call(functools.partial(tick, sections, splits), in_specs=[pl.Bl...  107 us
    pallas_call x1, Pallas kernels, shards(): pl.pallas_call(write_all, in_specs=[anywhere] * 7, out_specs=[pl.BlockSpe...  3.17 us

profile of v5, /device:TPU:11, one launch (start us, length us, event | category | flops | bytes accessed | tf_op | source)
XLA Modules:
  0.0 110.4 jit_solution(110661344309463322)
XLA Ops:
  0.6 106.6 %shard_map.144 = (bf16[64,8192]{1,0:T(8,128)(2,1)}, bf16[128,4096]{1,0:T(8,128)(2,1)}, bf16[128,512]{1,0:T(8,128)(2,1)}, bf16[128,512]{1,0:T(8,128)(2,1)}, bf16[...) custom-call(bf16[128,4096]{1,0:T(8,128)(2,1)} %bitcast.14, bf16[128,512]{1,0:T(8,128)(2,1)} %bitcast.20, ...), custom_call_target="tpu_custom_call" | custom-call | flops 1073741824 | bytes 8388608 | tf_op jit(solution)/shard_map/pallas_call | solution.py:449
  107.2 3.2 %shard_map.145 = (bf16[64,8192]{1,0:T(8,128)(2,1)}, bf16[128,4096]{1,0:T(8,128)(2,1)}, bf16[128,512]{1,0:T(8,128)(2,1)}, bf16[128,512]{1,0:T(8,128)(2,1)}, bf16[...) custom-call(bf16[64,8192]{1,0:T(8,128)(2,1)} %get-tuple-element.21.refs_0_, ...), custom_call_target="tpu_custom_call" | custom-call | tf_op jit(solution)/shard_map/pallas_call | solution.py:466

commit v6 on v5

--- a/solution.py
+++ b/solution.py
@@ -185,7 +185,7 @@
     send_pack_diag = remote(9, pack_dout, pack_din, mirror)
     send_score_diag = remote(10, score_dout, score_din, mirror)
     send_eq = [remote(12 + g, fwd_q.at[:, block(g)], evicted_q.at[:, block(g)], mirror) for g in range(kv_local)]
-    early, middle = (kv_local + 1) // 2, (3 * kv_local + 3) // 4
+    early = (kv_local + 1) // 2
     send_far = remote(11, fwd_ids, far_ids, mirror)
     send_out = []
     for offset in range(splits):
@@ -270,10 +270,27 @@
     for send in send_eq[:early]:
         send.start()
 
-    @pl.when(section_short)
+    @pl.when(jnp.logical_or(section_short, holder_short))
     def _():
         for send in send_eq[early:]:
             send.start()
+
+    def key_gradient(ref, diag_ref):
+        holder_masks = unpack_masks(*segment_sides(holder_ids))
+
+        def group(g):
+            total = jnp.zeros((tokens, HD), F32)
+            for h, (packed, on_diag) in enumerate(load_packed(g, ref, diag_ref)):
+                dscore = unpack(packed, on_diag, holder_masks).astype(LOW)
+                total = total + dot_tn(dscore, hq[:, head(g, h)])
+            gk[:, own(g)] = total.astype(LOW)
+
+        every_group(kv_local, group)
+
+    @pl.when(holder_short)
+    def _():
+        key_gradient(pack_out, pack_dout)
+        send_gk.start()
 
     for load in loads[4:]:
         load.wait()
@@ -318,8 +335,12 @@
         score_dout[...] = diag[...].astype(LOW)
         send_score.start()
         send_score_diag.start()
-        for send in send_eq[early:middle]:
-            send.start()
+
+        @pl.when(jnp.logical_not(holder_short))
+        def _():
+            for send in send_eq[early:]:
+                send.start()
+
 
     @pl.when(section_short)
     def _():
@@ -332,34 +353,13 @@
         every_group(kv_local, group)
         grad_v[...] = third_in[...]
 
-    def key_gradient(ref, diag_ref):
-        holder_masks = unpack_masks(*segment_sides(holder_ids))
-
-        def group(g):
-            total = jnp.zeros((tokens, HD), F32)
-            for h, (packed, on_diag) in enumerate(load_packed(g, ref, diag_ref)):
-                dscore = unpack(packed, on_diag, holder_masks).astype(LOW)
-                total = total + dot_tn(dscore, hq[:, head(g, h)])
-            gk[:, own(g)] = total.astype(LOW)
-
-        every_group(kv_local, group)
-
-    @pl.when(holder_short)
-    def _():
-        key_gradient(pack_out, pack_dout)
-
     @pl.when(jnp.logical_not(holder_short))
     def _():
         send_score.wait_recv()
         send_score_diag.wait_recv()
         key_gradient(score_in, score_din)
-
-    send_gk.start()
-
-    @pl.when(jnp.logical_not(section_short))
-    def _():
-        for send in send_eq[middle:]:
-            send.start()
+        send_gk.start()
+
 
     for send in [send_ek, send_ev, send_far]:
         send.wait_recv()

time: 111 us -> 108 us (0.973)
  the two profiles are of different devices: /device:TPU:11 before, /device:TPU:16 now
where the time goes in v6:
time: 108 us; the launch traced here: 107 us
  Pallas kernels  107 us (99%)
    pallas_call x1, Pallas kernels, shards(): pl.pallas_call(functools.partial(tick, sections, splits), in_specs=[pl.Bl...  104 us
    pallas_call x1, Pallas kernels, shards(): pl.pallas_call(write_all, in_specs=[anywhere] * 7, out_specs=[pl.BlockSpe...  3.17 us

profile of v6, /device:TPU:16, one launch (start us, length us, event | category | flops | bytes accessed | tf_op | source)
XLA Modules:
  0.0 107.5 jit_solution(7702955546484681715)
XLA Ops:
  0.6 103.6 %shard_map.144 = (bf16[64,8192]{1,0:T(8,128)(2,1)}, bf16[128,4096]{1,0:T(8,128)(2,1)}, bf16[128,512]{1,0:T(8,128)(2,1)}, bf16[128,512]{1,0:T(8,128)(2,1)}, bf16[...) custom-call(bf16[128,4096]{1,0:T(8,128)(2,1)} %bitcast.14, bf16[128,512]{1,0:T(8,128)(2,1)} %bitcast.20, ...), custom_call_target="tpu_custom_call" | custom-call | flops 1073741824 | bytes 8388608 | tf_op jit(solution)/shard_map/pallas_call | solution.py:449
  104.3 3.2 %shard_map.145 = (bf16[64,8192]{1,0:T(8,128)(2,1)}, bf16[128,4096]{1,0:T(8,128)(2,1)}, bf16[128,512]{1,0:T(8,128)(2,1)}, bf16[128,512]{1,0:T(8,128)(2,1)}, bf16[...) custom-call(bf16[64,8192]{1,0:T(8,128)(2,1)} %get-tuple-element.21.refs_0_, ...), custom_call_target="tpu_custom_call" | custom-call | tf_op jit(solution)/shard_map/pallas_call | solution.py:466

commit v7 on v6

--- a/solution.py
+++ b/solution.py
@@ -11,6 +11,7 @@
 KV = 8
 HD = 128
 GROUP = HQ // KV
+PARTS = 4
 SCALE = HD**-0.5
 LOW = jnp.bfloat16
 F32 = jnp.float32
@@ -418,8 +419,12 @@
     count = (len(refs) - 2) // 3
     here, there, rooms = refs[:count], refs[count : 2 * count], refs[2 * count : 3 * count]
     in_sem, out_sem = refs[3 * count :]
-    reads = [pltpu.make_async_copy(here[n], rooms[n], in_sem.at[n]) for n in range(count)]
-    writes = [pltpu.make_async_copy(rooms[n], there[n], out_sem.at[n]) for n in range(count)]
+    parts = []
+    for n in range(count):
+        step = here[n].shape[0] // PARTS if here[n].shape[0] % (16 * PARTS) == 0 else here[n].shape[0]
+        parts += [(n, pl.ds(at, step), at // step) for at in range(0, here[n].shape[0], step)]
+    reads = [pltpu.make_async_copy(here[n].at[r], rooms[n].at[r], in_sem.at[n, p]) for n, r, p in parts]
+    writes = [pltpu.make_async_copy(rooms[n].at[r], there[n].at[r], out_sem.at[n, p]) for n, r, p in parts]
     for read in reads:
         read.start()
     for read, write in zip(reads, writes):
@@ -468,7 +473,7 @@
         in_specs=[anywhere] * 7,
         out_specs=[pl.BlockSpec(memory_space=pltpu.HBM)] * 7,
         out_shape=[jax.ShapeDtypeStruct(result.shape, LOW) for result in results],
-        scratch_shapes=[pltpu.VMEM(result.shape, LOW) for result in results] + [pltpu.SemaphoreType.DMA((7,))] * 2,
+        scratch_shapes=[pltpu.VMEM(result.shape, LOW) for result in results] + [pltpu.SemaphoreType.DMA((7, PARTS))] * 2,
         compiler_params=pltpu.CompilerParams(vmem_limit_bytes=60 * 2**20),
     )(*results)
     return tuple(result[None] for result in results)

time: 108 us -> 108 us (level)
  no operation moved by 1% of the time
where the time goes in v7:
time: 108 us
  Pallas kernels  107 us (99%)
    pallas_call x1, Pallas kernels, shards(): pl.pallas_call(functools.partial(tick, sections, splits), in_specs=[pl.Bl...  104 us
    pallas_call x1, Pallas kernels, shards(): pl.pallas_call(write_all, in_specs=[anywhere] * 7, out_specs=[pl.BlockSpe...  3.29 us

profile of v7, /device:TPU:16, one launch (start us, length us, event | category | flops | bytes accessed | tf_op | source)
XLA Modules:
  0.0 107.6 jit_solution(10282532163867708043)
XLA Ops:
  0.6 103.6 %shard_map.144 = (bf16[64,8192]{1,0:T(8,128)(2,1)}, bf16[128,4096]{1,0:T(8,128)(2,1)}, bf16[128,512]{1,0:T(8,128)(2,1)}, bf16[128,512]{1,0:T(8,128)(2,1)}, bf16[...) custom-call(bf16[128,4096]{1,0:T(8,128)(2,1)} %bitcast.14, bf16[128,512]{1,0:T(8,128)(2,1)} %bitcast.20, ...), custom_call_target="tpu_custom_call" | custom-call | flops 1073741824 | bytes 8388608 | tf_op jit(solution)/shard_map/pallas_call | solution.py:454
  104.3 3.3 %shard_map.145 = (bf16[64,8192]{1,0:T(8,128)(2,1)}, bf16[128,4096]{1,0:T(8,128)(2,1)}, bf16[128,512]{1,0:T(8,128)(2,1)}, bf16[128,512]{1,0:T(8,128)(2,1)}, bf16[...) custom-call(bf16[64,8192]{1,0:T(8,128)(2,1)} %get-tuple-element.21.refs_0_, ...), custom_call_target="tpu_custom_call" | custom-call | tf_op jit(solution)/shard_map/pallas_call | solution.py:471
